TPU v7x, 32 devices: a whole 2x2x4 slice. The times are simulated.
32 devices in a mesh: segaz: 8 (over y, x, core), rad: 4 (over z).
Axes of the slice: x: 2, y: 2, z: 4, core: 2. Of those that a mesh axis runs over, the one named last changes fastest.
Arguments:
- state: float32 [5, 2048, 1024], P(None, 'segaz', 'rad'), may hold values from -6 to 6
- kappa: float32 [2048, 1024], P('segaz', 'rad'), may hold values from 0.1 to 1
- drop_src: float32 [5, 1048576], P(None, ('segaz', 'rad')), may hold values from -48 to 48
- drop_cell: int32 [1048576], P(('segaz', 'rad')), may hold values from 0 to 65535
- drop_count: int32 [32, 8], P(('segaz', 'rad')), may hold values from 1 to 5120, 32768 in all within a row
- part_map: int32 [8], replicated, may hold values from 0 to 7, as said below
- match_block: int32 [8], replicated, may hold values from 0 to 7, as said below
Outputs:
- new_state: float32 [5, 2048, 1024], P(None, 'segaz', 'rad')
Inputs may be any that keep to these rules, and one draw needn't show every extreme that they name: Each row of drop_count sums to 32768; a partition's droplet rows are grouped by destination in increasing segaz index: its first drop_count[p, 0] rows go to index 0, the next drop_count[p, 1] to index 1, and so on. Every row reaches the maximum. `part_map`: A permutation of the block ids. match_block[match_block[b]] = b and match_block[b] != b for every block b.
All inputs are finite; a program needn't handle non-finite values.
Results may differ from a plain program's by a relative error of at most 0.0003.
Values sent between devices are 32-bit elements; how exact they have to be, the bound alone decides.
No kernel may reach another device: no remote copies, remote signals or barrier semaphores. Data moves between devices by JAX's collectives and lax.ppermute only.
A program may use at most 128 MiB of HBM per device.

v0:
```python
import jax
import jax.numpy as jnp
from jax import lax
from jax.sharding import PartitionSpec as P

FW = 4
JL = 4


time_step = 0.25
layer_weights = (1.0, 0.6, 0.35, 0.2)


def extended(cells, sides, width):
    for axis, dim in sides:
        count = lax.axis_size(axis)
        ends = count - 1
        head = lax.slice_in_dim(cells, 0, width, axis=dim)
        tail = lax.slice_in_dim(cells, cells.shape[dim] - width, cells.shape[dim], axis=dim)
        cells = jnp.concatenate(
            [
                lax.ppermute(tail, axis, [(i, (i + 1) % count) for i in range(ends)]),
                cells,
                lax.ppermute(head, axis, [((i + 1) % count, i) for i in range(ends)]),
            ],
            axis=dim,
        )
    return cells


def filter_weights(half_width):
    offsets = jnp.arange(-half_width, half_width + 1).astype(jnp.float32)
    bell_curve = jnp.exp(-offsets * offsets / 8.0)
    return bell_curve / jnp.sum(bell_curve)


def smooth_axis(padded, half_width, axis_dim, length):
    weights = filter_weights(half_width)
    summed = weights[0] * lax.slice_in_dim(padded, 0, length, axis=axis_dim)
    for tap_index in range(1, 2 * half_width + 1):
        summed = summed + weights[tap_index] * lax.slice_in_dim(
            padded, tap_index, tap_index + length, axis=axis_dim
        )
    return summed


def laplace_nine(padded):
    centre = padded[:, 1:-1, 1:-1]
    edge_sum = (
        padded[:, 2:, 1:-1] + padded[:, :-2, 1:-1] + padded[:, 1:-1, 2:] + padded[:, 1:-1, :-2]
    )
    corners = padded[:, 2:, 2:] + padded[:, 2:, :-2] + padded[:, :-2, 2:] + padded[:, :-2, :-2]
    return (4.0 * edge_sum + corners - 20.0 * centre) / 6.0


def slot_rows(counts, targets, row_count, capacity):
    seg_count = counts.shape[0]
    group_ends = jnp.cumsum(counts)
    group_begin = group_ends - counts
    chosen = targets[:, None] == jnp.arange(seg_count, dtype=jnp.int32)[None, :]
    group_first = jnp.sum(jnp.where(chosen, group_begin[None, :], 0), axis=1)
    group_count = jnp.sum(jnp.where(chosen, counts[None, :], 0), axis=1)
    begin_row = jnp.minimum(group_first, row_count - capacity)
    row_index = begin_row[:, None] + jnp.arange(capacity, dtype=jnp.int32)[None, :]
    is_live = (row_index >= group_first[:, None]) & (
        row_index < (group_first + group_count)[:, None]
    )
    return (row_index, is_live)


def deposit(values, cell_ids, components, cell_total):
    return jnp.zeros((components, cell_total), jnp.float32).at[:, cell_ids].add(values)


def local(state, kappa, drop_src, drop_cell, drop_count, part_map, match_block):
    components, azim_cells, radial_cells = state.shape
    cell_total = azim_cells * radial_cells
    row_count = drop_src.shape[1]
    seg_count = lax.axis_size("segaz")
    capacity = 5 * row_count // (4 * seg_count)
    own_index = lax.axis_index("segaz")
    indices = jnp.arange(seg_count, dtype=jnp.int32)
    padded = extended(state, (("segaz", 1), ("rad", 2)), 1)
    diffusion = kappa[None] * laplace_nine(padded)
    my_block = jnp.sum(jnp.where(indices == own_index, part_map, 0))
    target = jnp.sum(jnp.where(indices == my_block, match_block, 0))
    partner = jnp.sum(jnp.where(part_map == target, indices, 0))
    face_rows = state[:, :JL, :]
    shards = lax.all_gather(face_rows[None], "segaz", axis=0, tiled=True)
    chosen = jnp.arange(shards.shape[0], dtype=jnp.int32) == partner
    partner_face = jnp.sum(jnp.where(chosen[:, None, None, None], shards, 0.0), axis=0)
    weights = jnp.array(layer_weights, jnp.float32)
    coupling = weights[None, :, None] * (partner_face - face_rows)
    junction = jnp.concatenate(
        [coupling, jnp.zeros((components, azim_cells - JL, radial_cells), jnp.float32)], axis=1
    )
    row_index, is_live = slot_rows(drop_count[0], indices, row_count, capacity)
    flat_index = row_index.reshape(-1)
    flat_live = is_live.reshape(-1)
    values = jnp.where(flat_live[None, :], drop_src[:, flat_index], 0.0)
    cell_ids = jnp.where(flat_live, drop_cell[flat_index], 0)[None, :]
    got_values, got_cells = (
        lax.all_to_all(values, "segaz", split_axis=1, concat_axis=1, tiled=True),
        lax.all_to_all(cell_ids, "segaz", split_axis=1, concat_axis=1, tiled=True),
    )
    source = deposit(got_values, got_cells[0], components, cell_total)
    source = source.reshape(components, azim_cells, radial_cells)
    wide_azim = extended(source, (("segaz", 1),), FW)
    smoothed = smooth_axis(wide_azim, FW, 1, azim_cells)
    wide_radial = extended(smoothed, (("rad", 2),), FW)
    filtered = smooth_axis(wide_radial, FW, 2, radial_cells)
    return state + time_step * (diffusion + junction + filtered)


def solution(mesh):
    return jax.shard_map(
        local,
        mesh=mesh,
        in_specs=(
            P(None, "segaz", "rad"),
            P("segaz", "rad"),
            P(None, ("segaz", "rad")),
            P(("segaz", "rad")),
            P(("segaz", "rad"), None),
            P(),
            P(),
        ),
        out_specs=P(None, "segaz", "rad"),
        check_vma=False,
    )
```

profile of v0, /device:TPU:19, one launch (start us, length us, event | category | flops | bytes accessed | tf_op | source)
XLA Modules:
  0.0 771.9 jit_solution(5196965062390579582)
XLA Ops:
  0.0 0.9 reduce-window_clone.1
  0.9 0.7 subtract_bitcast_fusion
  1.5 0.8 select_reduce_fusion.1
  2.9 225.5 %gather_fusion = s32[40960]{0:T(1024)S(1)} fusion(s32[32768]{0:T(1024)S(1)} %copy-done, s32[40960]{0:T(1024)S(1)} %broadcast_clamp_fusion), kind=kCustom, calls=%fused_computation | custom fusion | bytes 491520 | tf_op jit(solution)/shard_map/gather | solution.py:101
  228.4 1.0 and_select_fusion
  229.4 4.6 all-to-all-start
  234.0 2.3 collective-permute-start
  236.3 4.2 collective-permute-start.1
  240.6 0.7 fusion.64
  241.3 9.0 %copy.92 = f32[5,32768]{0,1:T(8,128)} copy(f32[5,32768]{1,0:T(8,128)S(1)} %copy-done.4) | data formatting | bytes 1310720 | tf_op args[2]
  250.3 141.7 %gather_fusion.1 = f32[40960,5]{1,0:T(8,128)} fusion(f32[5,32768]{0,1:T(8,128)} %copy.92, s32[40960]{0:T(1024)S(1)} %broadcast_clamp_fusion), kind=kCustom, calls=%fused_computation.1 | custom fusion | bytes 1802240 | tf_op jit(solution)/shard_map/gather | solution.py:100
  392.0 11.4 %copy.93 = f32[5,8,5120]{2,0,1:T(8,128)S(1)} copy(f32[5,8,5120]{0,2,1:T(8,128)} %bitcast.31) | data formatting | bytes 1638400 | tf_op jit(solution)/shard_map/gather | solution.py:100
  403.5 0.8 broadcast_multiply_fusion
  404.2 8.0 %all-gather = f32[40,4,256]{2,1,0:T(4,128)S(1)} all-gather(f32[5,4,256]{2,1,0:T(4,128)S(1)} %slice.171), channel_id=2, replica_groups=mesh['segaz'=8,'rad'=4] {'segaz'}, dimensions={0}, use_global_device_ids=true | all-gather | bytes 184320 | tf_op jit(solution)/shard_map/all_gather | solution.py:89
  412.3 0.6 fusion.61
  412.9 1.4 fusion.62
  414.2 1.3 fusion.63
  415.6 0.6 iota_compare_fusion.1
  416.2 1.3 broadcast_select_fusion
  417.7 0.7 broadcast_divide_fusion
  418.5 0.2 fusion.66
  418.8 0.5 copy.88
  419.3 2.1 collective-permute-start.2
  421.3 0.5 copy.90
  421.8 3.2 collective-permute-start.3
  425.0 4.4 all-to-all-start.1
  429.6 16.5 %all-to-all-done.1 = f32[5,8,5120]{2,0,1:T(8,128)S(1)} async-done(((f32[5,8,5120]{2,0,1:T(8,128)}), f32[5,8,5120]{2,0,1:T(8,128)S(1)}, u32[]{:S(2)}, u32[]{:S(2)}) %all-to-all-start.1) | async-done | bytes 819232 | tf_op jit(solution)/shard_map/all_to_all | solution.py:103
  446.0 10.1 %copy.94 = f32[40960,5]{1,0:T(8,128)} copy(f32[40960,5]{0,1:T(8,128)S(1)} %bitcast.32) | data formatting | bytes 1638400 | tf_op jit(solution)/shard_map/all_to_all | solution.py:103
  456.1 237.6 %scatter_custom_fusion = f32[5,65536]{0,1:T(8,128)} fusion(s32[40960]{0:T(1024)S(1)} %bitcast.38, f32[40960,5]{1,0:T(8,128)} %copy.94, f32[]{:T(128)} %constant.9.clone.1), kind=kCustom, calls=%fused_computation.3 | custom fusion | flops 204800 | bytes 1311232 | tf_op jit(solution)/shard_map/scatter-add | solution.py:72
  693.8 1.3 fusion.65
  695.1 0.2 copy.109
  695.2 8.6 %collective-permute-start.5 = (f32[5,4,256]{2,0,1:T(8,128)S(1)}, f32[5,4,256]{2,0,1:T(8,128)S(1)}, u32[]{:S(2)}, u32[]{:S(2)}) collective-permute-start(f32[5,4,256]{2,0,1:T(8,128)S(1)} %copy.109), channel_id=1, source_target_pairs={{4,0},{8,4},{12,8},{16,12},{20,16},{24,20},{28,24},{5,1},{9,5},{13... | collective-permute-start | bytes 61448 | tf_op jit(solution)/shard_map/ppermute | solution.py:24
  704.0 1.9 collective-permute-start.4
  705.9 0.7 fusion.69
  706.6 1.1 copy.89
  707.7 1.1 copy.91
  708.9 19.0 %copy.97 = f32[5,256,256]{2,1,0:T(8,128)S(1)} copy(f32[5,256,256]{0,2,1:T(8,128)} %bitcast.30) | data formatting | bytes 2621440 | tf_op jit(solution)/shard_map/reshape | solution.py:107
  727.9 7.5 fusion.28
  735.5 0.2 fusion.68
  735.7 0.8 copy-done.3
  736.5 0.3 copy.102
  736.8 9.0 %collective-permute-start.6 = (f32[5,256,4]{1,0,2:T(8,128)S(1)}, f32[5,256,4]{1,0,2:T(8,128)S(1)}, u32[]{:S(2)}, u32[]{:S(2)}) collective-permute-start(f32[5,256,4]{1,0,2:T(8,128)S(1)} %copy.102), channel_id=1, source_target_pairs={{0,1},{1,2},{2,3},{4,5},{5,6},{6,7},{8,9},{9,10},{10,11},{12,13},{... | collective-permute-start | bytes 61448 | tf_op jit(solution)/shard_map/ppermute | solution.py:22
  745.9 0.3 copy.104
  746.2 1.9 collective-permute-start.7
  748.1 3.3 pad_maximum_fusion
  751.4 1.1 copy.103
  752.6 1.1 copy.105
  753.7 18.1 %fusion.8 = f32[5,256,256]{2,1,0:T(8,128)} fusion(f32[5,256,256]{2,1,0:T(8,128)S(1)} %copy-done.2, f32[5,256,256]{2,1,0:T(8,128)} %copy-done.3, f32[5,256,4]{2,1,0:T(8,128)} %copy.105, f32[5,256,4]{2,1,0:T(8,128)} %copy.103, f32[5,258,257]{2,1,0:T(8,128)} %get-tuple-element.10, f32[5,258,257]{2,1,0:T(8,128)S(1)} %get-tuple-element.9, ...), kind=kLoop, calls=%fused_computation.32 | loop fusion | flops 13762560 | bytes 12130340 | tf_op jit(solution)/shard_map/add | solution.py:112
  (45 shorter events, 1.3 us)
Async XLA Ops:
  0.0 2.8 copy-start
  2.8 231.1 %copy-start.2 = (f32[5,256,256]{2,1,0:T(8,128)S(1)}, f32[5,256,256]{2,1,0:T(8,128)}, u32[]{:S(2)}) copy-start(f32[5,256,256]{2,1,0:T(8,128)} %param.8) | copy-start | bytes 3932164
  2.8 238.4 %copy-start.4 = (f32[5,32768]{1,0:T(8,128)S(1)}, f32[5,32768]{1,0:T(8,128)}, u32[]{:S(2)}) copy-start(f32[5,32768]{1,0:T(8,128)} %param.10) | copy-start | bytes 1966084
  229.4 195.7 %all-to-all-start = ((s32[1,8,5120]{2,0,1:T(1,128)}), s32[1,8,5120]{2,0,1:T(1,128)S(1)}, u32[]{:S(2)}, u32[]{:S(2)}) async-start(s32[1,8,5120]{2,0,1:T(1,128)} %and_select_fusion), calls=%async_computation | async-start | bytes 327680 | tf_op jit(solution)/shard_map/all_to_all | solution.py:104
  234.0 184.4 %collective-permute-start = (f32[5,1,256]{2,0,1:T(8,128)S(1)}, f32[5,1,256]{2,0,1:T(8,128)S(1)}, u32[]{:S(2)}, u32[]{:S(2)}) collective-permute-start(f32[5,1,256]{2,0,1:T(8,128)S(1)} %copy.106), channel_id=1, source_target_pairs={{4,0},{8,4},{12,8},{16,12},{20,16},{24,20},{28,24},{5,1},{9,5},{13... | collective-permute-start | bytes 15368 | tf_op jit(solution)/shard_map/ppermute | solution.py:24
  236.3 182.1 %collective-permute-start.1 = (f32[5,1,256]{2,0,1:T(8,128)S(1)}, f32[5,1,256]{2,0,1:T(8,128)S(1)}, u32[]{:S(2)}, u32[]{:S(2)}) collective-permute-start(f32[5,1,256]{2,0,1:T(8,128)S(1)} %copy.107), channel_id=1, source_target_pairs={{0,4},{4,8},{8,12},{12,16},{16,20},{20,24},{24,28},{1,5},{5,9},{9,... | collective-permute-start | bytes 15368 | tf_op jit(solution)/shard_map/ppermute | solution.py:22
  392.0 11.5 %copy-start.5 = (f32[256,256]{1,0:T(8,128)S(1)}, f32[256,256]{1,0:T(8,128)}, u32[]{:S(2)}) copy-start(f32[256,256]{1,0:T(8,128)} %param.9) | copy-start | bytes 786436
  392.0 20.3 %copy-start.8 = (s32[8]{0:T(128)S(1)}, s32[8]{0:T(128)}, u32[]{:S(2)}) copy-start(s32[8]{0:T(128)} %param.13) | copy-start | bytes 100
  392.0 20.9 %copy-start.7 = (s32[8]{0:T(128)S(1)}, s32[8]{0:T(128)}, u32[]{:S(2)}) copy-start(s32[8]{0:T(128)} %param.14) | copy-start | bytes 100
  416.2 1.4 copy-start.6
  419.3 287.4 %collective-permute-start.2 = (f32[5,258,1]{1,0,2:T(8,128)S(1)}, f32[5,258,1]{1,0,2:T(8,128)S(1)}, u32[]{:S(2)}, u32[]{:S(2)}) collective-permute-start(f32[5,258,1]{1,0,2:T(8,128)S(1)} %copy.88), channel_id=1, source_target_pairs={{1,0},{2,1},{3,2},{5,4},{6,5},{7,6},{9,8},{10,9},{11,10},{13,12},{... | collective-permute-start | bytes 15488 | tf_op jit(solution)/shard_map/ppermute | solution.py:24
  421.8 285.9 %collective-permute-start.3 = (f32[5,258,1]{1,0,2:T(8,128)S(1)}, f32[5,258,1]{1,0,2:T(8,128)S(1)}, u32[]{:S(2)}, u32[]{:S(2)}) collective-permute-start(f32[5,258,1]{1,0,2:T(8,128)S(1)} %copy.90), channel_id=1, source_target_pairs={{0,1},{1,2},{2,3},{4,5},{5,6},{6,7},{8,9},{9,10},{10,11},{12,13},{... | collective-permute-start | bytes 15488 | tf_op jit(solution)/shard_map/ppermute | solution.py:22
  425.0 21.0 %all-to-all-start.1 = ((f32[5,8,5120]{2,0,1:T(8,128)}), f32[5,8,5120]{2,0,1:T(8,128)S(1)}, u32[]{:S(2)}, u32[]{:S(2)}) async-start(f32[5,8,5120]{2,0,1:T(8,128)} %broadcast_select_fusion), calls=%async_computation.1 | async-start | bytes 2621440 | tf_op jit(solution)/shard_map/all_to_all | solution.py:103
  695.2 32.6 %collective-permute-start.5 = (f32[5,4,256]{2,0,1:T(8,128)S(1)}, f32[5,4,256]{2,0,1:T(8,128)S(1)}, u32[]{:S(2)}, u32[]{:S(2)}) collective-permute-start(f32[5,4,256]{2,0,1:T(8,128)S(1)} %copy.109), channel_id=1, source_target_pairs={{4,0},{8,4},{12,8},{16,12},{20,16},{24,20},{28,24},{5,1},{9,5},{13... | collective-permute-start | bytes 61448 | tf_op jit(solution)/shard_map/ppermute | solution.py:24
  704.0 23.9 %collective-permute-start.4 = (f32[5,4,256]{2,0,1:T(8,128)S(1)}, f32[5,4,256]{2,0,1:T(8,128)S(1)}, u32[]{:S(2)}, u32[]{:S(2)}) collective-permute-start(f32[5,4,256]{2,0,1:T(8,128)S(1)} %copy.108), channel_id=1, source_target_pairs={{0,4},{4,8},{8,12},{12,16},{16,20},{20,24},{24,28},{1,5},{5,9},{9,... | collective-permute-start | bytes 61448 | tf_op jit(solution)/shard_map/ppermute | solution.py:22
  735.4 1.1 copy-start.3
  736.8 14.6 %collective-permute-start.6 = (f32[5,256,4]{1,0,2:T(8,128)S(1)}, f32[5,256,4]{1,0,2:T(8,128)S(1)}, u32[]{:S(2)}, u32[]{:S(2)}) collective-permute-start(f32[5,256,4]{1,0,2:T(8,128)S(1)} %copy.102), channel_id=1, source_target_pairs={{0,1},{1,2},{2,3},{4,5},{5,6},{6,7},{8,9},{9,10},{10,11},{12,13},{... | collective-permute-start | bytes 61448 | tf_op jit(solution)/shard_map/ppermute | solution.py:22
  746.2 6.4 collective-permute-start.7
  753.7 18.1 %copy-start.1 = (s32[32768]{0:T(1024)S(1)}, s32[32768]{0:T(1024)}, u32[]{:S(2)}) copy-start(s32[32768]{0:T(1024)} %param.11) | copy-start | bytes 393220
where the time goes:
time: 778 us; the launch traced here: 772 us
  local copies, waits for them, and re-layouts  427 us (55%)
  other arithmetic  278 us (36%)
  starting transfers between devices  42.1 us (5%)
  waiting for transfers between devices  16.5 us (2%)
  blocking collectives  8.04 us (1%)
    scatter-add x1, other arithmetic, deposit(): jnp.zeros((components, cell_total), jnp.float32).at[:, cell_ids].add(values)  238 us
    gather x1, local copies, waits for them, and re-layouts, local(): cell_ids = jnp.where(flat_live, drop_cell[flat_index], 0)[None, :]  226 us
    gather x2, local copies, waits for them, and re-layouts, local(): values = jnp.where(flat_live[None, :], drop_src[:, flat_index], 0.0)  153 us
    reshape x1, local copies, waits for them, and re-layouts, local(): source = source.reshape(components, azim_cells, radial_cells)  19 us
    ppermute x4, starting transfers between devices, extended(): lax.ppermute(tail, axis, [(i, (i + 1) % count) for i in range(ends)])  18.3 us
    add x1, other arithmetic, local(): return state + time_step * (diffusion + junction + filtered)  18.1 us
    all_to_all x1, waiting for transfers between devices, local(): lax.all_to_all(values, 'segaz', split_axis=1, concat_axis=1, tiled=True)  16.5 us
  transfers between devices with their start and end apart: 10, of which 1 were waited for; matrix products, arithmetic and copies ran while one was open for 58% of the time, Pallas kernels for 0%

commit v1 on v0

v1 whole, which is shorter than its diff:
```python
import functools

import jax
import jax.numpy as jnp
from jax import lax
from jax.experimental import pallas as pl
from jax.experimental.pallas import tpu as pltpu
from jax.sharding import PartitionSpec as P

FW = 4
JL = 4
LANES = 128

time_step = 0.25
layer_weights = (1.0, 0.6, 0.35, 0.2)


def extended(cells, sides, width):
    for axis, dim in sides:
        count = lax.axis_size(axis)
        ends = count - 1
        head = lax.slice_in_dim(cells, 0, width, axis=dim)
        tail = lax.slice_in_dim(cells, cells.shape[dim] - width, cells.shape[dim], axis=dim)
        cells = jnp.concatenate(
            [
                lax.ppermute(tail, axis, [(i, (i + 1) % count) for i in range(ends)]),
                cells,
                lax.ppermute(head, axis, [((i + 1) % count, i) for i in range(ends)]),
            ],
            axis=dim,
        )
    return cells


def filter_weights(half_width):
    offsets = jnp.arange(-half_width, half_width + 1).astype(jnp.float32)
    bell_curve = jnp.exp(-offsets * offsets / 8.0)
    return bell_curve / jnp.sum(bell_curve)


def smooth_axis(padded, half_width, axis_dim, length):
    weights = filter_weights(half_width)
    summed = weights[0] * lax.slice_in_dim(padded, 0, length, axis=axis_dim)
    for tap_index in range(1, 2 * half_width + 1):
        summed = summed + weights[tap_index] * lax.slice_in_dim(
            padded, tap_index, tap_index + length, axis=axis_dim
        )
    return summed


def laplace_nine(padded):
    centre = padded[:, 1:-1, 1:-1]
    edge_sum = (
        padded[:, 2:, 1:-1] + padded[:, :-2, 1:-1] + padded[:, 1:-1, 2:] + padded[:, 1:-1, :-2]
    )
    corners = padded[:, 2:, 2:] + padded[:, 2:, :-2] + padded[:, :-2, 2:] + padded[:, :-2, :-2]
    return (4.0 * edge_sum + corners - 20.0 * centre) / 6.0


def pack_kernel(cap_tiles, base, count_ref, src_ref, cell_ref, state_ref, out_ref):
    seg_count = out_ref.shape[0]
    components = src_ref.shape[0]
    fields = components + 1
    tile_count = cell_ref.shape[0]
    lane = lax.broadcasted_iota(jnp.int32, (8, LANES), 1)
    sub = lax.broadcasted_iota(jnp.int32, (8, LANES), 0)

    def slot(g, begin):
        count = count_ref[0, g]
        first = begin // LANES
        shift = begin % LANES
        turn = (LANES - shift) % LANES

        def rolled(i):
            t = jnp.minimum(first + i, tile_count - 1)
            src = src_ref[:, pl.ds(pl.multiple_of(t * LANES, LANES), LANES)]
            cell = cell_ref[pl.ds(t, 1), :].astype(jnp.float32)
            both = jnp.concatenate([src, cell, jnp.zeros((8 - fields, LANES), jnp.float32)], axis=0)
            return pltpu.roll(both, turn, 1)

        for v in range(components):
            for half in range(2):
                out_ref[g, 8 * v + 4 * half : 8 * v + 4 * half + JL, :] = state_ref[
                    v, 0:JL, half * LANES : (half + 1) * LANES
                ]
        head = rolled(0)
        for i in range(cap_tiles):
            tail = rolled(i + 1)
            rows = jnp.where(lane < LANES - shift, head, tail)
            dead = (sub == components) & (lane >= count - i * LANES)
            rows = jnp.where(dead, -1.0 - count.astype(jnp.float32), rows)
            out_ref[g, base + fields * i : base + fields * (i + 1), :] = rows[:fields]
            head = tail
        return begin + count

    lax.fori_loop(0, seg_count, slot, jnp.int32(0))


def deposit_kernel(cap_tiles, base, step, got_ref, out_ref):
    seg_count = got_ref.shape[0]
    components = out_ref.shape[0]
    azim, radial = out_ref.shape[1:]
    fields = components + 1
    width = step * LANES
    end = base + fields * cap_tiles
    lane = lax.broadcasted_iota(jnp.int32, (1, LANES), 1)
    cells = lax.broadcasted_iota(jnp.int32, (azim, width), 0).astype(jnp.float32).astype(jnp.bfloat16)
    out_ref[...] = jnp.zeros(out_ref.shape, jnp.float32)

    def slot(s, carry):
        tail = got_ref[s, end - 1 : end, :]
        mark = jnp.sum(jnp.where(lane == LANES - 1, tail, 0.0)).astype(jnp.int32)
        count = jnp.where(mark >= 0, cap_tiles * LANES, -1 - mark)

        def chunk(j, carry):
            rows = got_ref[s, pl.ds(pl.multiple_of(base + fields * step * j, 8), fields * step), :]

            def field(k):
                return jnp.concatenate(
                    [rows[fields * q + k : fields * q + k + 1] for q in range(step)], axis=1
                )

            ids = field(components)
            a = jnp.floor(ids * (1.0 / radial))
            b = (ids - radial * a).astype(jnp.bfloat16)
            in_b = jnp.where(cells == b, jnp.bfloat16(1), jnp.bfloat16(0))
            in_a = cells == a.astype(jnp.bfloat16)
            right = jnp.concatenate([in_b, in_b], axis=1)
            for v in range(components):
                values = field(v)
                high = values.astype(jnp.bfloat16)
                low = (values - high.astype(jnp.float32)).astype(jnp.bfloat16)
                left = jnp.concatenate(
                    [jnp.where(in_a, high, jnp.bfloat16(0)), jnp.where(in_a, low, jnp.bfloat16(0))],
                    axis=1,
                )
                out_ref[v] += lax.dot_general(
                    left, right, (((1,), (1,)), ((), ())), preferred_element_type=jnp.float32
                )
            return carry

        return lax.fori_loop(0, (count + width - 1) // width, chunk, carry)

    lax.fori_loop(0, seg_count, slot, 0)


def local(state, kappa, drop_src, drop_cell, drop_count, part_map, match_block):
    components, azim_cells, radial_cells = state.shape
    row_count = drop_src.shape[1]
    seg_count = lax.axis_size("segaz")
    capacity = 5 * row_count // (4 * seg_count)
    cap_tiles = capacity // LANES
    step = 4 if cap_tiles % 4 == 0 else 2
    base = 8 * components
    fields = components + 1
    slot_rows = -(-(base + fields * cap_tiles) // 8) * 8
    own_index = lax.axis_index("segaz")
    indices = jnp.arange(seg_count, dtype=jnp.int32)
    vmem = pl.BlockSpec(memory_space=pltpu.VMEM)
    smem = pl.BlockSpec(memory_space=pltpu.SMEM)
    sends = pl.pallas_call(
        functools.partial(pack_kernel, cap_tiles, base),
        out_shape=jax.ShapeDtypeStruct((seg_count, slot_rows, LANES), jnp.float32),
        in_specs=[smem, vmem, vmem, vmem],
        out_specs=vmem,
        compiler_params=pltpu.CompilerParams(vmem_limit_bytes=48 << 20),
    )(drop_count, drop_src, drop_cell.reshape(-1, LANES), state)
    got = lax.all_to_all(sends, "segaz", split_axis=0, concat_axis=0, tiled=True)
    source = pl.pallas_call(
        functools.partial(deposit_kernel, cap_tiles, base, step),
        out_shape=jax.ShapeDtypeStruct(state.shape, jnp.float32),
        in_specs=[vmem],
        out_specs=vmem,
        compiler_params=pltpu.CompilerParams(vmem_limit_bytes=48 << 20),
    )(got)

    padded = extended(state, (("segaz", 1), ("rad", 2)), 1)
    diffusion = kappa[None] * laplace_nine(padded)
    my_block = jnp.sum(jnp.where(indices == own_index, part_map, 0))
    target = jnp.sum(jnp.where(indices == my_block, match_block, 0))
    partner = jnp.sum(jnp.where(part_map == target, indices, 0))
    face_rows = state[:, :JL, :]
    partner_face = lax.dynamic_index_in_dim(got, partner, 0, keepdims=False)[:base]
    partner_face = partner_face.reshape(components, 2, JL, LANES).transpose(0, 2, 1, 3).reshape(face_rows.shape)
    weights = jnp.array(layer_weights, jnp.float32)
    coupling = weights[None, :, None] * (partner_face - face_rows)
    junction = jnp.concatenate(
        [coupling, jnp.zeros((components, azim_cells - JL, radial_cells), jnp.float32)], axis=1
    )
    wide_azim = extended(source, (("segaz", 1),), FW)
    smoothed = smooth_axis(wide_azim, FW, 1, azim_cells)
    wide_radial = extended(smoothed, (("rad", 2),), FW)
    filtered = smooth_axis(wide_radial, FW, 2, radial_cells)
    return state + time_step * (diffusion + junction + filtered)


def solution(mesh):
    return jax.shard_map(
        local,
        mesh=mesh,
        in_specs=(
            P(None, "segaz", "rad"),
            P("segaz", "rad"),
            P(None, ("segaz", "rad")),
            P(("segaz", "rad")),
            P(("segaz", "rad"), None),
            P(),
            P(),
        ),
        out_specs=P(None, "segaz", "rad"),
        check_vma=False,
    )
```

time: 778 us -> 156 us (0.20)
  local copies, waits for them, and re-layouts: 427 us -> 17.3 us
  other arithmetic: 278 us -> 33.9 us
  Pallas kernels: 0 us -> 59 us
  waiting for transfers between devices: 16.5 us -> 4.66 us
  blocking collectives: 8.04 us -> 0 us
    gather x3 -> x0, local copies, waits for them, and re-layouts: 379 us -> none  [the longest x1 226 us: local(): cell_ids = jnp.where(flat_live, drop_cell[flat_index], 0)[None, :]]
    scatter-add x1 -> x0, other arithmetic: 238 us -> none  [deposit(): jnp.zeros((components, cell_total), jnp.float32).at[:, cell_ids].add(values)]
    pallas_call x0 -> x2, Pallas kernels: none -> 59 us  [the longest x1 57.1 us: local(): pl.pallas_call(functools.partial(deposit_kernel, cap_tiles, base, step),...]
    reshape x1 -> x0, local copies, waits for them, and re-layouts: 19 us -> none  [local(): source = source.reshape(components, azim_cells, radial_cells)]
    all_to_all x2 -> x1, waiting for transfers between devices: 16.5 us -> 0.01 us  [local(): lax.all_to_all(sends, 'segaz', split_axis=0, concat_axis=0, tiled=True)]
    all_to_all x1 -> x0, local copies, waits for them, and re-layouts: 10.1 us -> none  [local(): lax.all_to_all(values, 'segaz', split_axis=1, concat_axis=1, tiled=True)]
    all_gather x1 -> x0, blocking collectives: 8.04 us -> none  [local(): shards = lax.all_gather(face_rows[None], 'segaz', axis=0, tiled=True)]
  transfers between devices with their start and end apart: 10 -> 9, of which waited for: 1 -> 2; matrix products, arithmetic and copies ran while one was open for 58% -> 10% of each run, Pallas kernels for 0% -> 1%
where the time goes in v1:
time: 156 us; the launch traced here: 153 us
  Pallas kernels  59 us (38%)
  starting transfers between devices  36.5 us (23%)
  other arithmetic  33.9 us (22%)
  local copies, waits for them, and re-layouts  17.3 us (11%)
  waiting for transfers between devices  4.66 us (3%)
  between operations  2.12 us (1%)
    pallas_call x1, Pallas kernels, local(): pl.pallas_call(functools.partial(deposit_kernel, cap_tiles, base, step),...  57.1 us
    ppermute x4, starting transfers between devices, extended(): lax.ppermute(tail, axis, [(i, (i + 1) % count) for i in range(ends)])  22.3 us
    add x1, other arithmetic, local(): return state + time_step * (diffusion + junction + filtered)  17.6 us
    ppermute x4, starting transfers between devices, extended(): lax.ppermute(head, axis, [((i + 1) % count, i) for i in range(ends)])  9.46 us
    add x1, other arithmetic, smooth_axis(): summed + weights[tap_index] * lax.slice_in_dim(padded, tap_index, tap_ind...  7.27 us
    unnamed x24, local copies, waits for them, and re-layouts  5.2 us
    all_to_all x1, starting transfers between devices, local(): lax.all_to_all(sends, 'segaz', split_axis=0, concat_axis=0, tiled=True)  4.67 us
    slice x5, local copies, waits for them, and re-layouts, extended(): lax.slice_in_dim(cells, cells.shape[dim] - width, cells.shape[dim], axis=...  4.02 us
  transfers between devices with their start and end apart: 9, of which 2 were waited for; matrix products, arithmetic and copies ran while one was open for 10% of the time, Pallas kernels for 1%

profile of v1, /device:TPU:19, one launch (start us, length us, event | category | flops | bytes accessed | tf_op | source)
XLA Modules:
  0.0 153.5 jit_solution(1282434921572579261)
XLA Ops:
  0.0 0.8 fusion.60
  0.8 3.7 %collective-permute-start.1 = (f32[5,1,256]{2,1,0:T(1,128)S(1)}, f32[5,1,256]{2,1,0:T(1,128)S(1)}, u32[]{:S(2)}, u32[]{:S(2)}) collective-permute-start(f32[5,1,256]{2,1,0:T(1,128)S(1)} %get-tuple-element.9), channel_id=1, source_target_pairs={{0,4},{4,8},{8,12},{12,16},{16,20},{20,24},{24,28},{1,5},{5,9},{9,... | collective-permute-start | bytes 15368 | tf_op jit(solution)/shard_map/ppermute | solution.py:26
  4.5 1.9 %collective-permute-start = (f32[5,1,256]{2,1,0:T(1,128)S(1)}, f32[5,1,256]{2,1,0:T(1,128)S(1)}, u32[]{:S(2)}, u32[]{:S(2)}) collective-permute-start(f32[5,1,256]{2,1,0:T(1,128)S(1)} %get-tuple-element.10), channel_id=1, source_target_pairs={{4,0},{8,4},{12,8},{16,12},{20,16},{24,20},{28,24},{5,1},{9,5},{13... | collective-permute-start | bytes 15368 | tf_op jit(solution)/shard_map/ppermute | solution.py:28
  6.4 0.0 copy-start
  6.4 1.3 copy-done
  7.7 1.2 copy-done.3
  9.0 0.9 copy-done.4
  9.9 0.7 copy-done.5
  10.5 1.9 %shard_map.82 = f32[8,280,128]{2,1,0:T(8,128)S(1)} custom-call(s32[1,8]{1,0:T(1,128)S(1)} %copy-done.5, f32[5,32768]{1,0:T(8,128)S(1)} %copy-done.3, s32[256,128]{1,0:T(8,128)S(1)} %bitcast.15, f32[5,256,256]{2,1,0:T(8,128)S(1)} %copy-done), custom_call_target="tpu_custom_call" | custom-call | tf_op jit(solution)/shard_map/pallas_call | solution.py:161
  12.4 0.0 copy-start.2
  12.4 1.0 copy-done.2
  13.4 4.7 %all-to-all-start = ((f32[8,280,128]{2,1,0:T(8,128)}), f32[8,280,128]{2,1,0:T(8,128)S(1)}, u32[]{:S(2)}, u32[]{:S(2)}) async-start(f32[8,280,128]{2,1,0:T(8,128)} %copy-done.2), calls=%async_computation | async-start | bytes 2293760 | tf_op jit(solution)/shard_map/all_to_all | solution.py:168
  18.1 0.6 fusion.58
  18.7 0.7 broadcast_multiply_fusion
  19.4 0.7 fusion.55
  20.1 0.6 broadcast_divide_fusion
  20.7 0.7 fusion.63
  21.3 1.3 fusion.56
  22.6 0.0 collective-permute-done.1
  22.6 0.1 pad_maximum_fusion.1
  22.8 1.0 fusion.59
  23.8 1.4 copy.9
  25.2 0.3 copy.11
  25.6 3.2 %collective-permute-start.3 = (f32[5,258,1]{1,2,0:T(1,128)S(1)}, f32[5,258,1]{1,2,0:T(1,128)S(1)}, u32[]{:S(2)}, u32[]{:S(2)}) collective-permute-start(f32[5,258,1]{1,2,0:T(1,128)S(1)} %copy.11), channel_id=1, source_target_pairs={{0,1},{1,2},{2,3},{4,5},{5,6},{6,7},{8,9},{9,10},{10,11},{12,13},{... | collective-permute-start | bytes 15488 | tf_op jit(solution)/shard_map/ppermute | solution.py:26
  28.8 2.1 %collective-permute-start.2 = (f32[5,258,1]{1,2,0:T(1,128)S(1)}, f32[5,258,1]{1,2,0:T(1,128)S(1)}, u32[]{:S(2)}, u32[]{:S(2)}) collective-permute-start(f32[5,258,1]{1,2,0:T(1,128)S(1)} %copy.9), channel_id=1, source_target_pairs={{1,0},{2,1},{3,2},{5,4},{6,5},{7,6},{9,8},{10,9},{11,10},{13,12},{... | collective-permute-start | bytes 15488 | tf_op jit(solution)/shard_map/ppermute | solution.py:28
  30.9 1.3 fusion.57
  34.1 0.0 collective-permute-done.2
  34.1 0.3 copy.10
  34.4 1.1 copy.12
  35.5 3.7 %pad_maximum_fusion = (f32[5,258,257]{2,1,0:T(8,128)}, f32[5,258,257]{2,1,0:T(8,128)}) fusion(f32[5,258,1]{2,1,0:T(8,128)S(1)} %copy.10, f32[5,1,256]{2,1,0:T(1,128)S(1)} %collective-permute-done, f32[5,256,256]{2,1,0:T(8,128)S(1)} %copy-done.1, f32[5,1,256]{2,1,0:T(1,128)S(1)} %collective-permute-done.1, f32[5,258,1]{2,1,0:T(8,128)} %copy.12), kind=kLoop, calls=%fused_computation.18 | loop fusion | flops 1989180 | bytes 3983520 | tf_op jit(solution)/shard_map/concatenate | solution.py:24
  39.2 0.0 all-to-all-done.got_ref
  39.2 57.1 %shard_map.83 = f32[5,256,256]{2,1,0:T(8,128)S(1)} custom-call(f32[8,280,128]{2,1,0:T(8,128)S(1)} %all-to-all-done.got_ref), custom_call_target="tpu_custom_call" | custom-call | tf_op jit(solution)/shard_map/pallas_call | solution.py:169
  96.4 12.1 %collective-permute-start.4 = (f32[5,4,256]{2,1,0:T(4,128)S(1)}, f32[5,4,256]{2,1,0:T(4,128)S(1)}, u32[]{:S(2)}, u32[]{:S(2)}) collective-permute-start(f32[5,4,256]{2,1,0:T(4,128)S(1)} %get-tuple-element.13), channel_id=1, source_target_pairs={{0,4},{4,8},{8,12},{12,16},{16,20},{20,24},{24,28},{1,5},{5,9},{9,... | collective-permute-start | bytes 61448 | tf_op jit(solution)/shard_map/ppermute | solution.py:26
  108.5 2.4 %collective-permute-start.5 = (f32[5,4,256]{2,1,0:T(4,128)S(1)}, f32[5,4,256]{2,1,0:T(4,128)S(1)}, u32[]{:S(2)}, u32[]{:S(2)}) collective-permute-start(f32[5,4,256]{2,1,0:T(4,128)S(1)} %get-tuple-element.14), channel_id=1, source_target_pairs={{4,0},{8,4},{12,8},{16,12},{20,16},{24,20},{28,24},{5,1},{9,5},{13... | collective-permute-start | bytes 61448 | tf_op jit(solution)/shard_map/ppermute | solution.py:28
  111.0 0.0 collective-permute-done.4
  111.0 3.5 %collective-permute-done.5 = f32[5,4,256]{2,1,0:T(4,128)S(1)} collective-permute-done((f32[5,4,256]{2,1,0:T(4,128)S(1)}, f32[5,4,256]{2,1,0:T(4,128)S(1)}, u32[]{:S(2)}, u32[]{:S(2)}) %collective-permute-start.5) | collective-permute-done | bytes 20512 | tf_op jit(solution)/shard_map/ppermute | solution.py:28
  114.5 7.3 %fusion.26 = f32[5,256,256]{2,1,0:T(8,128)S(1)} fusion(f32[5,4,256]{2,1,0:T(4,128)S(1)} %collective-permute-done.5, f32[5,4,256]{2,1,0:T(4,128)S(1)} %collective-permute-done.4, f32[5,256,256]{2,1,0:T(8,128)S(1)} %shard_map.83, f32[]{:T(128)} %bitcast.12, f32[]{:T(128)} %bitcast.11, f32[]{:T(128)} %bitcast.10, f32[]{:T(128)} %bitcast.9, f32[]{:T(128)} %bitcast.8, ...), kind=kLoop, calls=%fused_computation.47 | loop fusion | flops 8192000 | bytes 2662436 | tf_op jit(solution)/shard_map/add | solution.py:45
  121.8 1.4 fusion.61
  123.2 0.1 copy-done.7
  123.3 1.5 copy.13
  124.7 1.3 copy.15
  126.1 3.0 %collective-permute-start.7 = (f32[5,256,4]{1,2,0:T(4,128)S(1)}, f32[5,256,4]{1,2,0:T(4,128)S(1)}, u32[]{:S(2)}, u32[]{:S(2)}) collective-permute-start(f32[5,256,4]{1,2,0:T(4,128)S(1)} %copy.15), channel_id=1, source_target_pairs={{1,0},{2,1},{3,2},{5,4},{6,5},{7,6},{9,8},{10,9},{11,10},{13,12},{... | collective-permute-start | bytes 61448 | tf_op jit(solution)/shard_map/ppermute | solution.py:28
  129.1 3.3 %collective-permute-start.6 = (f32[5,256,4]{1,2,0:T(4,128)S(1)}, f32[5,256,4]{1,2,0:T(4,128)S(1)}, u32[]{:S(2)}, u32[]{:S(2)}) collective-permute-start(f32[5,256,4]{1,2,0:T(4,128)S(1)} %copy.13), channel_id=1, source_target_pairs={{0,1},{1,2},{2,3},{4,5},{5,6},{6,7},{8,9},{9,10},{10,11},{12,13},{... | collective-permute-start | bytes 61448 | tf_op jit(solution)/shard_map/ppermute | solution.py:26
  132.4 0.1 subtract_multiply_fusion
  132.5 1.1 collective-permute-done.6
  133.6 1.1 copy.14
  134.8 1.1 copy.16
  135.9 17.6 %fusion.6 = f32[5,256,256]{2,1,0:T(8,128)} fusion(f32[5,256,256]{2,1,0:T(8,128)S(1)} %copy-done.1, f32[5,256,256]{2,1,0:T(8,128)} %copy-done.7, f32[5,256,4]{2,1,0:T(8,128)} %copy.16, f32[5,256,4]{2,1,0:T(8,128)} %copy.14, f32[5,258,257]{2,1,0:T(8,128)} %get-tuple-element.8, f32[5,258,257]{2,1,0:T(8,128)S(1)} %copy-done.6, ...), kind=kLoop, calls=%fused_computation.27 | loop fusion | flops 13762560 | bytes 12130340 | tf_op jit(solution)/shard_map/add | solution.py:194
  (21 shorter events, 0.1 us)
Async XLA Ops:
  0.8 21.8 %collective-permute-start.1 = (f32[5,1,256]{2,1,0:T(1,128)S(1)}, f32[5,1,256]{2,1,0:T(1,128)S(1)}, u32[]{:S(2)}, u32[]{:S(2)}) collective-permute-start(f32[5,1,256]{2,1,0:T(1,128)S(1)} %get-tuple-element.9), channel_id=1, source_target_pairs={{0,4},{4,8},{8,12},{12,16},{16,20},{20,24},{24,28},{1,5},{5,9},{9,... | collective-permute-start | bytes 15368 | tf_op jit(solution)/shard_map/ppermute | solution.py:26
  4.5 18.1 %collective-permute-start = (f32[5,1,256]{2,1,0:T(1,128)S(1)}, f32[5,1,256]{2,1,0:T(1,128)S(1)}, u32[]{:S(2)}, u32[]{:S(2)}) collective-permute-start(f32[5,1,256]{2,1,0:T(1,128)S(1)} %get-tuple-element.10), channel_id=1, source_target_pairs={{4,0},{8,4},{12,8},{16,12},{20,16},{24,20},{28,24},{5,1},{9,5},{13... | collective-permute-start | bytes 15368 | tf_op jit(solution)/shard_map/ppermute | solution.py:28
  6.4 1.3 copy-start
  7.7 1.2 copy-start.3
  9.0 0.9 copy-start.4
  9.9 0.7 copy-start.5
  12.4 1.0 copy-start.2
  13.4 5.3 %copy-start.8 = (f32[256,256]{1,0:T(8,128)S(1)}, f32[256,256]{1,0:T(8,128)}, u32[]{:S(2)}) copy-start(f32[256,256]{1,0:T(8,128)} %param.9) | copy-start | bytes 786436
  13.4 6.0 %copy-start.11 = (s32[8]{0:T(128)S(1)}, s32[8]{0:T(128)}, u32[]{:S(2)}) copy-start(s32[8]{0:T(128)} %param.13) | copy-start | bytes 100
  13.4 7.9 %copy-start.10 = (s32[8]{0:T(128)S(1)}, s32[8]{0:T(128)}, u32[]{:S(2)}) copy-start(s32[8]{0:T(128)} %param.14) | copy-start | bytes 100
  13.4 9.2 %copy-start.1 = (f32[5,256,256]{2,1,0:T(8,128)S(1)}, f32[5,256,256]{2,1,0:T(8,128)}, u32[]{:S(2)}) copy-start(f32[5,256,256]{2,1,0:T(8,128)} %state_ref.1) | copy-start | bytes 3932164
  13.4 25.8 %all-to-all-start = ((f32[8,280,128]{2,1,0:T(8,128)}), f32[8,280,128]{2,1,0:T(8,128)S(1)}, u32[]{:S(2)}, u32[]{:S(2)}) async-start(f32[8,280,128]{2,1,0:T(8,128)} %copy-done.2), calls=%async_computation | async-start | bytes 2293760 | tf_op jit(solution)/shard_map/all_to_all | solution.py:168
  25.6 8.8 %collective-permute-start.3 = (f32[5,258,1]{1,2,0:T(1,128)S(1)}, f32[5,258,1]{1,2,0:T(1,128)S(1)}, u32[]{:S(2)}, u32[]{:S(2)}) collective-permute-start(f32[5,258,1]{1,2,0:T(1,128)S(1)} %copy.11), channel_id=1, source_target_pairs={{0,1},{1,2},{2,3},{4,5},{5,6},{6,7},{8,9},{9,10},{10,11},{12,13},{... | collective-permute-start | bytes 15488 | tf_op jit(solution)/shard_map/ppermute | solution.py:26
  28.8 5.3 %collective-permute-start.2 = (f32[5,258,1]{1,2,0:T(1,128)S(1)}, f32[5,258,1]{1,2,0:T(1,128)S(1)}, u32[]{:S(2)}, u32[]{:S(2)}) collective-permute-start(f32[5,258,1]{1,2,0:T(1,128)S(1)} %copy.9), channel_id=1, source_target_pairs={{1,0},{2,1},{3,2},{5,4},{6,5},{7,6},{9,8},{10,9},{11,10},{13,12},{... | collective-permute-start | bytes 15488 | tf_op jit(solution)/shard_map/ppermute | solution.py:28
  96.4 14.6 %collective-permute-start.4 = (f32[5,4,256]{2,1,0:T(4,128)S(1)}, f32[5,4,256]{2,1,0:T(4,128)S(1)}, u32[]{:S(2)}, u32[]{:S(2)}) collective-permute-start(f32[5,4,256]{2,1,0:T(4,128)S(1)} %get-tuple-element.13), channel_id=1, source_target_pairs={{0,4},{4,8},{8,12},{12,16},{16,20},{20,24},{24,28},{1,5},{5,9},{9,... | collective-permute-start | bytes 61448 | tf_op jit(solution)/shard_map/ppermute | solution.py:26
  108.5 6.0 %collective-permute-start.5 = (f32[5,4,256]{2,1,0:T(4,128)S(1)}, f32[5,4,256]{2,1,0:T(4,128)S(1)}, u32[]{:S(2)}, u32[]{:S(2)}) collective-permute-start(f32[5,4,256]{2,1,0:T(4,128)S(1)} %get-tuple-element.14), channel_id=1, source_target_pairs={{4,0},{8,4},{12,8},{16,12},{20,16},{24,20},{28,24},{5,1},{9,5},{13... | collective-permute-start | bytes 61448 | tf_op jit(solution)/shard_map/ppermute | solution.py:28
  121.8 1.5 copy-start.7
  123.3 9.2 %copy-start.9 = (f32[4]{0:T(128)S(1)}, f32[4]{0:T(128)}, u32[]{:S(2)}) copy-start(f32[4]{0:T(128)} %constant.32.clone) | copy-start | bytes 52
  123.3 12.6 %copy-start.6 = (f32[5,258,257]{2,1,0:T(8,128)S(1)}, f32[5,258,257]{2,1,0:T(8,128)}, u32[]{:S(2)}) copy-start(f32[5,258,257]{2,1,0:T(8,128)} %get-tuple-element.7) | copy-start | bytes 3978364
  126.1 8.7 %collective-permute-start.7 = (f32[5,256,4]{1,2,0:T(4,128)S(1)}, f32[5,256,4]{1,2,0:T(4,128)S(1)}, u32[]{:S(2)}, u32[]{:S(2)}) collective-permute-start(f32[5,256,4]{1,2,0:T(4,128)S(1)} %copy.15), channel_id=1, source_target_pairs={{1,0},{2,1},{3,2},{5,4},{6,5},{7,6},{9,8},{10,9},{11,10},{13,12},{... | collective-permute-start | bytes 61448 | tf_op jit(solution)/shard_map/ppermute | solution.py:28
  129.1 4.5 %collective-permute-start.6 = (f32[5,256,4]{1,2,0:T(4,128)S(1)}, f32[5,256,4]{1,2,0:T(4,128)S(1)}, u32[]{:S(2)}, u32[]{:S(2)}) collective-permute-start(f32[5,256,4]{1,2,0:T(4,128)S(1)} %copy.13), channel_id=1, source_target_pairs={{0,1},{1,2},{2,3},{4,5},{5,6},{6,7},{8,9},{9,10},{10,11},{12,13},{... | collective-permute-start | bytes 61448 | tf_op jit(solution)/shard_map/ppermute | solution.py:26

commit v2 on v1

--- a/solution.py
+++ b/solution.py
@@ -10,6 +10,11 @@
 FW = 4
 JL = 4
 LANES = 128
+WINDOW = 64
+ROUNDS = 2
+UNROLL = 8
+WIDE = False
+STEP = 4
 
 time_step = 0.25
 layer_weights = (1.0, 0.6, 0.35, 0.2)
@@ -57,13 +62,43 @@
     return (4.0 * edge_sum + corners - 20.0 * centre) / 6.0
 
 
-def pack_kernel(cap_tiles, base, count_ref, src_ref, cell_ref, state_ref, out_ref):
-    seg_count = out_ref.shape[0]
+def comparators(count):
+    size = 1 << (count - 1).bit_length()
+    pairs = []
+    p = 1
+    while p < size:
+        k = p
+        while k >= 1:
+            for j in range(k % p, size - k, 2 * k):
+                for i in range(min(k, size - j - k)):
+                    if (i + j) // (2 * p) == (i + j + k) // (2 * p) and i + j + k < count:
+                        pairs.append((i + j, i + j + k))
+            k //= 2
+        p *= 2
+    return pairs
+
+
+def sort_rows(tiles):
+    pairs = comparators(len(tiles))
+    for low, high in pairs:
+        swap = tiles[high][-1] < tiles[low][-1]
+        first = [jnp.where(swap, y, x) for x, y in zip(tiles[low], tiles[high])]
+        second = [jnp.where(swap, x, y) for x, y in zip(tiles[low], tiles[high])]
+        tiles[low], tiles[high] = first, second
+    return tiles
+
+
+def pack_kernel(cap_tiles, step, base, count_ref, src_ref, cell_ref, state_ref, out_ref, held_ref):
     components = src_ref.shape[0]
     fields = components + 1
     tile_count = cell_ref.shape[0]
+    radial = state_ref.shape[2]
+    azim = state_ref.shape[1]
+    slot_rows = base + 8 + -(-fields * cap_tiles // 8) * 8
+    seg_count = out_ref.shape[0] // slot_rows
     lane = lax.broadcasted_iota(jnp.int32, (8, LANES), 1)
     sub = lax.broadcasted_iota(jnp.int32, (8, LANES), 0)
+    none = float(azim * radial)
 
     def slot(g, begin):
         count = count_ref[0, g]
@@ -78,9 +113,10 @@
             both = jnp.concatenate([src, cell, jnp.zeros((8 - fields, LANES), jnp.float32)], axis=0)
             return pltpu.roll(both, turn, 1)
 
+        row = g * slot_rows
         for v in range(components):
             for half in range(2):
-                out_ref[g, 8 * v + 4 * half : 8 * v + 4 * half + JL, :] = state_ref[
+                out_ref[pl.ds(row + 8 * v + 4 * half, JL), :] = state_ref[
                     v, 0:JL, half * LANES : (half + 1) * LANES
                 ]
         head = rolled(0)
@@ -88,60 +124,131 @@
             tail = rolled(i + 1)
             rows = jnp.where(lane < LANES - shift, head, tail)
             dead = (sub == components) & (lane >= count - i * LANES)
-            rows = jnp.where(dead, -1.0 - count.astype(jnp.float32), rows)
-            out_ref[g, base + fields * i : base + fields * (i + 1), :] = rows[:fields]
+            rows = jnp.where(dead, none, rows)
+            held_ref[g // 8, i, pl.ds(g % 8, 8, stride=8), :] = rows
             head = tail
         return begin + count
 
     lax.fori_loop(0, seg_count, slot, jnp.int32(0))
 
-
-def deposit_kernel(cap_tiles, base, step, got_ref, out_ref):
-    seg_count = got_ref.shape[0]
+    def group(h, carry):
+        tiles = [
+            [held_ref[h, i, 8 * f : 8 * f + 8, :] for f in range(fields)] for i in range(cap_tiles)
+        ]
+        tiles = sort_rows(tiles)
+        for again in range(ROUNDS - 1):
+            tiles = [[pltpu.roll(x, (37 * i) % LANES, 1) for x in tiles[i]] for i in range(cap_tiles)]
+            tiles = sort_rows(tiles)
+        row = h * 8 * slot_rows
+        bounds = jnp.zeros((8, LANES), jnp.float32)
+        for j in range(cap_tiles // step):
+            keys = [tiles[i][-1] for i in range(step * j, step * j + step)]
+            least = jnp.min(keys[0], axis=1, keepdims=True)
+            most = keys[0]
+            most = jnp.where(most < none, most, -1.0)
+            for key in keys[1:]:
+                most = jnp.maximum(most, jnp.where(key < none, key, -1.0))
+            most = jnp.max(most, axis=1, keepdims=True)
+            bounds = jnp.where(lane == 2 * j, jnp.floor(least * (1.0 / radial)), bounds)
+            bounds = jnp.where(lane == 2 * j + 1, jnp.floor(most * (1.0 / radial)), bounds)
+        out_ref[pl.ds(row + slot_rows - 1, 8, stride=slot_rows), :] = bounds
+        for i in range(cap_tiles):
+            for f in range(fields):
+                out_ref[pl.ds(row + base + fields * i + f, 8, stride=slot_rows), :] = tiles[i][f]
+        return carry
+
+    lax.fori_loop(0, seg_count // 8, group, 0)
+
+
+def deposit_kernel(cap_tiles, base, step, got_ref, out_ref, bound_ref, sum_ref, limit_ref, work_ref, sem):
+    seg_count, slot_rows, _ = got_ref.shape
     components = out_ref.shape[0]
     azim, radial = out_ref.shape[1:]
     fields = components + 1
     width = step * LANES
-    end = base + fields * cap_tiles
-    lane = lax.broadcasted_iota(jnp.int32, (1, LANES), 1)
-    cells = lax.broadcasted_iota(jnp.int32, (azim, width), 0).astype(jnp.float32).astype(jnp.bfloat16)
-    out_ref[...] = jnp.zeros(out_ref.shape, jnp.float32)
-
-    def slot(s, carry):
-        tail = got_ref[s, end - 1 : end, :]
-        mark = jnp.sum(jnp.where(lane == LANES - 1, tail, 0.0)).astype(jnp.int32)
-        count = jnp.where(mark >= 0, cap_tiles * LANES, -1 - mark)
-
-        def chunk(j, carry):
-            rows = got_ref[s, pl.ds(pl.multiple_of(base + fields * step * j, 8), fields * step), :]
-
-            def field(k):
-                return jnp.concatenate(
-                    [rows[fields * q + k : fields * q + k + 1] for q in range(step)], axis=1
-                )
-
-            ids = field(components)
-            a = jnp.floor(ids * (1.0 / radial))
-            b = (ids - radial * a).astype(jnp.bfloat16)
-            in_b = jnp.where(cells == b, jnp.bfloat16(1), jnp.bfloat16(0))
-            in_a = cells == a.astype(jnp.bfloat16)
-            right = jnp.concatenate([in_b, in_b], axis=1)
+    chunk_count = cap_tiles // step
+    for s in range(seg_count):
+        bound_ref[s : s + 1, :] = got_ref[s, slot_rows - 1 : slot_rows, :].astype(jnp.int32)
+    copy = pltpu.make_async_copy(bound_ref, limit_ref, sem)
+    copy.start()
+    sum_ref[...] = jnp.zeros(sum_ref.shape, jnp.float32)
+    cells = lax.broadcasted_iota(jnp.int32, (radial, width), 0).astype(jnp.float32).astype(jnp.bfloat16)
+    near = lax.broadcasted_iota(jnp.int32, (WINDOW, width), 0).astype(jnp.float32).astype(jnp.bfloat16)
+    copy.wait()
+
+    def listed(s, total):
+        for j in range(chunk_count):
+            least = limit_ref[s, 2 * j] // 8 * 8
+            most = limit_ref[s, 2 * j + 1]
+
+            def add(start, total):
+                work_ref[0, total] = s
+                work_ref[1, total] = fields * step * j
+                work_ref[2, total] = start
+                return total + 1
+
+            work_ref[0, total] = s
+            work_ref[1, total] = fields * step * j
+            work_ref[2, total] = least
+            total = jnp.where(most >= 0, total + 1, total)
+            total = lax.while_loop(
+                lambda c: c[0] <= most,
+                lambda c: (c[0] + WINDOW, add(c[0], c[1])),
+                (least + WINDOW, total),
+            )[1]
+        return total
+
+    total = lax.fori_loop(0, seg_count, listed, jnp.int32(0))
+    for u in range(UNROLL - 1):
+        work_ref[0, total + u] = 0
+        work_ref[1, total + u] = 0
+        work_ref[2, total + u] = azim
+
+    def product(t):
+        s = work_ref[0, t]
+        begin = work_ref[1, t]
+        start = pl.multiple_of(work_ref[2, t], 8)
+        rows = got_ref[s, pl.ds(pl.multiple_of(base + begin, 8 if step % 4 == 0 else 4), fields * step), :]
+
+        def field(k):
+            return jnp.concatenate(
+                [rows[fields * q + k : fields * q + k + 1] for q in range(step)], axis=1
+            )
+
+        ids = field(components)
+        a = jnp.floor(ids * (1.0 / radial))
+        b = (ids - radial * a).astype(jnp.bfloat16)
+        right = jnp.where(cells == b, jnp.bfloat16(1), jnp.bfloat16(0))
+        in_a = near == (a - start.astype(jnp.float32)).astype(jnp.bfloat16)
+        highs, lows = [], []
+        for v in range(components):
+            values = field(v)
+            high = values.astype(jnp.bfloat16)
+            low = (values - high.astype(jnp.float32)).astype(jnp.bfloat16)
+            highs.append(jnp.where(in_a, high, jnp.bfloat16(0)))
+            lows.append(jnp.where(in_a, low, jnp.bfloat16(0)))
+        if WIDE:
+            left = jnp.concatenate([jnp.concatenate(highs, axis=0), jnp.concatenate(lows, axis=0)], axis=1)
+            part = lax.dot_general(
+                left, jnp.concatenate([right, right], axis=1), (((1,), (1,)), ((), ())), preferred_element_type=jnp.float32
+            )
+        else:
+            left = jnp.concatenate(highs + lows, axis=0)
+            part = lax.dot_general(
+                left, right, (((1,), (1,)), ((), ())), preferred_element_type=jnp.float32
+            )
+            part = part[: components * WINDOW] + part[components * WINDOW :]
+        return start, part
+
+    def several(t, carry):
+        done = [product(t * UNROLL + u) for u in range(UNROLL)]
+        for start, part in done:
             for v in range(components):
-                values = field(v)
-                high = values.astype(jnp.bfloat16)
-                low = (values - high.astype(jnp.float32)).astype(jnp.bfloat16)
-                left = jnp.concatenate(
-                    [jnp.where(in_a, high, jnp.bfloat16(0)), jnp.where(in_a, low, jnp.bfloat16(0))],
-                    axis=1,
-                )
-                out_ref[v] += lax.dot_general(
-                    left, right, (((1,), (1,)), ((), ())), preferred_element_type=jnp.float32
-                )
-            return carry
-
-        return lax.fori_loop(0, (count + width - 1) // width, chunk, carry)
-
-    lax.fori_loop(0, seg_count, slot, 0)
+                sum_ref[v, pl.ds(start, WINDOW), :] += part[v * WINDOW : (v + 1) * WINDOW]
+        return carry
+
+    lax.fori_loop(0, (total + UNROLL - 1) // UNROLL, several, 0)
+    out_ref[...] = sum_ref[:, :azim, :]
 
 
 def local(state, kappa, drop_src, drop_cell, drop_count, part_map, match_block):
@@ -150,27 +257,36 @@
     seg_count = lax.axis_size("segaz")
     capacity = 5 * row_count // (4 * seg_count)
     cap_tiles = capacity // LANES
-    step = 4 if cap_tiles % 4 == 0 else 2
+    step = STEP if cap_tiles % STEP == 0 else 2
     base = 8 * components
     fields = components + 1
-    slot_rows = -(-(base + fields * cap_tiles) // 8) * 8
+    slot_rows = base + 8 + -(-fields * cap_tiles // 8) * 8
     own_index = lax.axis_index("segaz")
     indices = jnp.arange(seg_count, dtype=jnp.int32)
     vmem = pl.BlockSpec(memory_space=pltpu.VMEM)
     smem = pl.BlockSpec(memory_space=pltpu.SMEM)
     sends = pl.pallas_call(
-        functools.partial(pack_kernel, cap_tiles, base),
-        out_shape=jax.ShapeDtypeStruct((seg_count, slot_rows, LANES), jnp.float32),
+        functools.partial(pack_kernel, cap_tiles, step, base),
+        out_shape=jax.ShapeDtypeStruct((seg_count * slot_rows, LANES), jnp.float32),
         in_specs=[smem, vmem, vmem, vmem],
         out_specs=vmem,
+        scratch_shapes=[pltpu.VMEM((seg_count // 8, cap_tiles, 64, LANES), jnp.float32)],
         compiler_params=pltpu.CompilerParams(vmem_limit_bytes=48 << 20),
     )(drop_count, drop_src, drop_cell.reshape(-1, LANES), state)
+    sends = sends.reshape(seg_count, slot_rows, LANES)
     got = lax.all_to_all(sends, "segaz", split_axis=0, concat_axis=0, tiled=True)
     source = pl.pallas_call(
         functools.partial(deposit_kernel, cap_tiles, base, step),
         out_shape=jax.ShapeDtypeStruct(state.shape, jnp.float32),
         in_specs=[vmem],
         out_specs=vmem,
+        scratch_shapes=[
+            pltpu.VMEM((seg_count, LANES), jnp.int32),
+            pltpu.VMEM((components, azim_cells + WINDOW, radial_cells), jnp.float32),
+            pltpu.SMEM((seg_count, LANES), jnp.int32),
+            pltpu.SMEM((3, seg_count * (cap_tiles // step) * (azim_cells // WINDOW + 2) + UNROLL), jnp.int32),
+            pltpu.SemaphoreType.DMA(()),
+        ],
         compiler_params=pltpu.CompilerParams(vmem_limit_bytes=48 << 20),
     )(got)
 

time: 156 us -> 115 us (0.74)
  Pallas kernels: 59 us -> 28 us
  starting transfers between devices: 36.5 us -> 26 us
  waiting for transfers between devices: 4.66 us -> 6.49 us
    pallas_call x1, Pallas kernels: 57.1 us -> 23.9 us  [local(): pl.pallas_call(functools.partial(deposit_kernel, cap_tiles, base, step),...]
    ppermute x4, starting transfers between devices: 22.3 us -> 11.2 us  [extended(): lax.ppermute(tail, axis, [(i, (i + 1) % count) for i in range(ends)])]
    pallas_call x1, Pallas kernels: 1.89 us -> 4.14 us  [local(): pl.pallas_call(functools.partial(pack_kernel, cap_tiles, step, base), out...]
    ppermute x4, waiting for transfers between devices: 1.12 us -> 2.87 us  [extended(): lax.ppermute(tail, axis, [(i, (i + 1) % count) for i in range(ends)])]
  transfers between devices with their start and end apart: 9 -> 9, of which waited for: 2 -> 2; matrix products, arithmetic and copies ran while one was open for 10% -> 13% of each run, Pallas kernels for 1% -> 4%
where the time goes in v2:
time: 115 us; the launch traced here: 114 us
  other arithmetic  33.9 us (29%)
  Pallas kernels  28 us (24%)
  starting transfers between devices  26 us (23%)
  local copies, waits for them, and re-layouts  17.3 us (15%)
  waiting for transfers between devices  6.49 us (6%)
  between operations  2.12 us (2%)
    pallas_call x1, Pallas kernels, local(): pl.pallas_call(functools.partial(deposit_kernel, cap_tiles, base, step),...  23.9 us
    add x1, other arithmetic, local(): return state + time_step * (diffusion + junction + filtered)  17.6 us
    ppermute x4, starting transfers between devices, extended(): lax.ppermute(tail, axis, [(i, (i + 1) % count) for i in range(ends)])  11.2 us
    ppermute x4, starting transfers between devices, extended(): lax.ppermute(head, axis, [((i + 1) % count, i) for i in range(ends)])  10.1 us
    add x1, other arithmetic, smooth_axis(): summed + weights[tap_index] * lax.slice_in_dim(padded, tap_index, tap_ind...  7.27 us
    unnamed x24, local copies, waits for them, and re-layouts  5.21 us
    all_to_all x1, starting transfers between devices, local(): lax.all_to_all(sends, 'segaz', split_axis=0, concat_axis=0, tiled=True)  4.67 us
    pallas_call x1, Pallas kernels, local(): pl.pallas_call(functools.partial(pack_kernel, cap_tiles, step, base), out...  4.14 us
  transfers between devices with their start and end apart: 9, of which 2 were waited for; matrix products, arithmetic and copies ran while one was open for 13% of the time, Pallas kernels for 4%

profile of v2, /device:TPU:19, one launch (start us, length us, event | category | flops | bytes accessed | tf_op | source)
XLA Modules:
  0.0 113.9 jit_solution(1946232702174088689)
XLA Ops:
  0.0 0.8 fusion.60
  0.8 3.7 %collective-permute-start.1 = (f32[5,1,256]{2,1,0:T(1,128)S(1)}, f32[5,1,256]{2,1,0:T(1,128)S(1)}, u32[]{:S(2)}, u32[]{:S(2)}) collective-permute-start(f32[5,1,256]{2,1,0:T(1,128)S(1)} %get-tuple-element.9), channel_id=1, source_target_pairs={{0,4},{4,8},{8,12},{12,16},{16,20},{20,24},{24,28},{1,5},{5,9},{9,... | collective-permute-start | bytes 15368 | tf_op jit(solution)/shard_map/ppermute | solution.py:31
  4.5 1.9 %collective-permute-start = (f32[5,1,256]{2,1,0:T(1,128)S(1)}, f32[5,1,256]{2,1,0:T(1,128)S(1)}, u32[]{:S(2)}, u32[]{:S(2)}) collective-permute-start(f32[5,1,256]{2,1,0:T(1,128)S(1)} %get-tuple-element.10), channel_id=1, source_target_pairs={{4,0},{8,4},{12,8},{16,12},{20,16},{24,20},{28,24},{5,1},{9,5},{13... | collective-permute-start | bytes 15368 | tf_op jit(solution)/shard_map/ppermute | solution.py:33
  6.4 0.0 copy-start
  6.4 1.3 %copy-done = f32[5,256,256]{2,1,0:T(8,128)S(1)} copy-done((f32[5,256,256]{2,1,0:T(8,128)S(1)}, f32[5,256,256]{2,1,0:T(8,128)}, u32[]{:S(2)}) %copy-start) | copy-done | bytes 1310744
  7.7 1.2 %copy-done.3 = f32[5,32768]{1,0:T(8,128)S(1)} copy-done((f32[5,32768]{1,0:T(8,128)S(1)}, f32[5,32768]{1,0:T(8,128)}, u32[]{:S(2)}) %copy-start.3) | copy-done | bytes 655384
  9.0 0.9 copy-done.4
  9.9 0.7 copy-done.5
  10.5 4.1 %shard_map.82 = f32[2304,128]{1,0:T(8,128)S(1)} custom-call(s32[1,8]{1,0:T(1,128)S(1)} %copy-done.5, f32[5,32768]{1,0:T(8,128)S(1)} %copy-done.3, s32[256,128]{1,0:T(8,128)S(1)} %bitcast.17, f32[5,256,256]{2,1,0:T(8,128)S(1)} %copy-done), custom_call_target="tpu_custom_call" | custom-call | tf_op jit(solution)/shard_map/pallas_call | solution.py:268
  14.7 0.0 copy-start.2
  14.7 1.0 copy-done.2
  15.7 4.7 %all-to-all-start = ((f32[8,288,128]{2,1,0:T(8,128)}), f32[8,288,128]{2,1,0:T(8,128)S(1)}, u32[]{:S(2)}, u32[]{:S(2)}) async-start(f32[8,288,128]{2,1,0:T(8,128)} %bitcast.16), calls=%async_computation | async-start | bytes 2359296 | tf_op jit(solution)/shard_map/all_to_all | solution.py:277
  20.4 0.6 fusion.58
  21.0 0.7 broadcast_multiply_fusion
  21.7 0.7 fusion.55
  22.4 0.6 broadcast_divide_fusion
  22.9 0.7 fusion.63
  23.6 1.3 %fusion.56 = s32[]{:T(128)} fusion(s32[8]{0:T(128)S(1)} %copy-done.10, s32[]{:T(128)} %fusion.55), kind=kLoop, calls=%fused_computation.96 | loop fusion | flops 23 | bytes 40 | tf_op jit(solution)/shard_map/reduce_sum | solution.py:296
  24.9 0.1 pad_maximum_fusion.1
  25.0 1.0 fusion.59
  26.1 1.4 %copy.9 = f32[5,258,1]{1,2,0:T(1,128)S(1)} copy(f32[5,258,1]{2,1,0:T(8,128)} %get-tuple-element.5) | data formatting | bytes 10320 | tf_op jit(solution)/shard_map/slice | solution.py:27
  27.5 0.3 copy.11
  27.8 3.2 %collective-permute-start.3 = (f32[5,258,1]{1,2,0:T(1,128)S(1)}, f32[5,258,1]{1,2,0:T(1,128)S(1)}, u32[]{:S(2)}, u32[]{:S(2)}) collective-permute-start(f32[5,258,1]{1,2,0:T(1,128)S(1)} %copy.11), channel_id=1, source_target_pairs={{0,1},{1,2},{2,3},{4,5},{5,6},{6,7},{8,9},{9,10},{10,11},{12,13},{... | collective-permute-start | bytes 15488 | tf_op jit(solution)/shard_map/ppermute | solution.py:31
  31.1 2.1 %collective-permute-start.2 = (f32[5,258,1]{1,2,0:T(1,128)S(1)}, f32[5,258,1]{1,2,0:T(1,128)S(1)}, u32[]{:S(2)}, u32[]{:S(2)}) collective-permute-start(f32[5,258,1]{1,2,0:T(1,128)S(1)} %copy.9), channel_id=1, source_target_pairs={{1,0},{2,1},{3,2},{5,4},{6,5},{7,6},{9,8},{10,9},{11,10},{13,12},{... | collective-permute-start | bytes 15488 | tf_op jit(solution)/shard_map/ppermute | solution.py:33
  33.1 1.3 %fusion.57 = s32[]{:T(128)} fusion(s32[8]{0:T(128)S(1)} %copy-done.11, s32[]{:T(128)} %fusion.56), kind=kLoop, calls=%fused_computation.97 | loop fusion | flops 23 | bytes 40 | tf_op jit(solution)/shard_map/reduce_sum | solution.py:297
  36.3 0.0 collective-permute-done.2
  36.4 0.3 copy.10
  36.6 1.1 copy.12
  37.8 3.7 %pad_maximum_fusion = (f32[5,258,257]{2,1,0:T(8,128)}, f32[5,258,257]{2,1,0:T(8,128)}) fusion(f32[5,258,1]{2,1,0:T(8,128)S(1)} %copy.10, f32[5,1,256]{2,1,0:T(1,128)S(1)} %collective-permute-done, f32[5,256,256]{2,1,0:T(8,128)S(1)} %copy-done.1, f32[5,1,256]{2,1,0:T(1,128)S(1)} %collective-permute-done.1, f32[5,258,1]{2,1,0:T(8,128)} %copy.12), kind=kLoop, calls=%fused_computation.18 | loop fusion | flops 1989180 | bytes 3983520 | tf_op jit(solution)/shard_map/concatenate | solution.py:29
  41.5 0.0 all-to-all-done.got_ref
  41.5 23.9 %shard_map.83 = f32[5,256,256]{2,1,0:T(8,128)S(1)} custom-call(f32[8,288,128]{2,1,0:T(8,128)S(1)} %all-to-all-done.got_ref), custom_call_target="tpu_custom_call" | custom-call | tf_op jit(solution)/shard_map/pallas_call | solution.py:278
  65.4 2.4 %collective-permute-start.4 = (f32[5,4,256]{2,1,0:T(4,128)S(1)}, f32[5,4,256]{2,1,0:T(4,128)S(1)}, u32[]{:S(2)}, u32[]{:S(2)}) collective-permute-start(f32[5,4,256]{2,1,0:T(4,128)S(1)} %get-tuple-element.13), channel_id=1, source_target_pairs={{0,4},{4,8},{8,12},{12,16},{16,20},{20,24},{24,28},{1,5},{5,9},{9,... | collective-permute-start | bytes 61448 | tf_op jit(solution)/shard_map/ppermute | solution.py:31
  67.8 2.4 %collective-permute-start.5 = (f32[5,4,256]{2,1,0:T(4,128)S(1)}, f32[5,4,256]{2,1,0:T(4,128)S(1)}, u32[]{:S(2)}, u32[]{:S(2)}) collective-permute-start(f32[5,4,256]{2,1,0:T(4,128)S(1)} %get-tuple-element.14), channel_id=1, source_target_pairs={{4,0},{8,4},{12,8},{16,12},{20,16},{24,20},{28,24},{5,1},{9,5},{13... | collective-permute-start | bytes 61448 | tf_op jit(solution)/shard_map/ppermute | solution.py:33
  70.2 0.0 collective-permute-done.4
  70.2 3.6 %collective-permute-done.5 = f32[5,4,256]{2,1,0:T(4,128)S(1)} collective-permute-done((f32[5,4,256]{2,1,0:T(4,128)S(1)}, f32[5,4,256]{2,1,0:T(4,128)S(1)}, u32[]{:S(2)}, u32[]{:S(2)}) %collective-permute-start.5) | collective-permute-done | bytes 20512 | tf_op jit(solution)/shard_map/ppermute | solution.py:33
  73.8 7.3 %fusion.26 = f32[5,256,256]{2,1,0:T(8,128)S(1)} fusion(f32[5,4,256]{2,1,0:T(4,128)S(1)} %collective-permute-done.5, f32[5,4,256]{2,1,0:T(4,128)S(1)} %collective-permute-done.4, f32[5,256,256]{2,1,0:T(8,128)S(1)} %shard_map.83, f32[]{:T(128)} %bitcast.13, f32[]{:T(128)} %bitcast.12, f32[]{:T(128)} %bitcast.11, f32[]{:T(128)} %bitcast.10, f32[]{:T(128)} %bitcast.9, ...), kind=kLoop, calls=%fused_computation.47 | loop fusion | flops 8192000 | bytes 2662436 | tf_op jit(solution)/shard_map/add | solution.py:50
  81.1 1.4 %fusion.61 = (f32[5,256,4]{2,1,0:T(8,128)}, f32[5,256,4]{2,1,0:T(8,128)}) fusion(f32[5,256,256]{2,1,0:T(8,128)S(1)} %fusion.26), kind=kLoop, calls=%fused_computation.103 | loop fusion | bytes 81920 | tf_op jit(solution)/shard_map/slice | solution.py:28
  82.5 0.1 copy-done.7
  82.6 1.5 %copy.13 = f32[5,256,4]{1,2,0:T(4,128)S(1)} copy(f32[5,256,4]{2,1,0:T(8,128)} %get-tuple-element.11) | data formatting | bytes 40960 | tf_op jit(solution)/shard_map/slice | solution.py:28
  84.1 1.3 %copy.15 = f32[5,256,4]{1,2,0:T(4,128)S(1)} copy(f32[5,256,4]{2,1,0:T(8,128)} %get-tuple-element.12) | data formatting | bytes 40960 | tf_op jit(solution)/shard_map/slice | solution.py:27
  85.4 3.8 %collective-permute-start.7 = (f32[5,256,4]{1,2,0:T(4,128)S(1)}, f32[5,256,4]{1,2,0:T(4,128)S(1)}, u32[]{:S(2)}, u32[]{:S(2)}) collective-permute-start(f32[5,256,4]{1,2,0:T(4,128)S(1)} %copy.15), channel_id=1, source_target_pairs={{1,0},{2,1},{3,2},{5,4},{6,5},{7,6},{9,8},{10,9},{11,10},{13,12},{... | collective-permute-start | bytes 61448 | tf_op jit(solution)/shard_map/ppermute | solution.py:33
  89.2 1.9 %collective-permute-start.6 = (f32[5,256,4]{1,2,0:T(4,128)S(1)}, f32[5,256,4]{1,2,0:T(4,128)S(1)}, u32[]{:S(2)}, u32[]{:S(2)}) collective-permute-start(f32[5,256,4]{1,2,0:T(4,128)S(1)} %copy.13), channel_id=1, source_target_pairs={{0,1},{1,2},{2,3},{4,5},{5,6},{6,7},{8,9},{9,10},{10,11},{12,13},{... | collective-permute-start | bytes 61448 | tf_op jit(solution)/shard_map/ppermute | solution.py:31
  91.1 0.1 subtract_multiply_fusion
  91.2 2.9 %collective-permute-done.6 = f32[5,256,4]{1,2,0:T(4,128)S(1)} collective-permute-done((f32[5,256,4]{1,2,0:T(4,128)S(1)}, f32[5,256,4]{1,2,0:T(4,128)S(1)}, u32[]{:S(2)}, u32[]{:S(2)}) %collective-permute-start.6) | collective-permute-done | bytes 20512 | tf_op jit(solution)/shard_map/ppermute | solution.py:31
  94.0 1.1 copy.14
  95.1 0.0 collective-permute-done.7
  95.1 1.1 copy.16
  96.3 17.6 %fusion.6 = f32[5,256,256]{2,1,0:T(8,128)} fusion(f32[5,256,256]{2,1,0:T(8,128)S(1)} %copy-done.1, f32[5,256,256]{2,1,0:T(8,128)} %copy-done.7, f32[5,256,4]{2,1,0:T(8,128)} %copy.16, f32[5,256,4]{2,1,0:T(8,128)} %copy.14, f32[5,258,257]{2,1,0:T(8,128)} %get-tuple-element.8, f32[5,258,257]{2,1,0:T(8,128)S(1)} %copy-done.6, ...), kind=kLoop, calls=%fused_computation.27 | loop fusion | flops 13762560 | bytes 12130340 | tf_op jit(solution)/shard_map/add | solution.py:310
  (21 shorter events, 0.1 us)
Async XLA Ops:
  0.8 24.1 %collective-permute-start.1 = (f32[5,1,256]{2,1,0:T(1,128)S(1)}, f32[5,1,256]{2,1,0:T(1,128)S(1)}, u32[]{:S(2)}, u32[]{:S(2)}) collective-permute-start(f32[5,1,256]{2,1,0:T(1,128)S(1)} %get-tuple-element.9), channel_id=1, source_target_pairs={{0,4},{4,8},{8,12},{12,16},{16,20},{20,24},{24,28},{1,5},{5,9},{9,... | collective-permute-start | bytes 15368 | tf_op jit(solution)/shard_map/ppermute | solution.py:31
  4.5 20.4 %collective-permute-start = (f32[5,1,256]{2,1,0:T(1,128)S(1)}, f32[5,1,256]{2,1,0:T(1,128)S(1)}, u32[]{:S(2)}, u32[]{:S(2)}) collective-permute-start(f32[5,1,256]{2,1,0:T(1,128)S(1)} %get-tuple-element.10), channel_id=1, source_target_pairs={{4,0},{8,4},{12,8},{16,12},{20,16},{24,20},{28,24},{5,1},{9,5},{13... | collective-permute-start | bytes 15368 | tf_op jit(solution)/shard_map/ppermute | solution.py:33
  6.4 1.3 %copy-start = (f32[5,256,256]{2,1,0:T(8,128)S(1)}, f32[5,256,256]{2,1,0:T(8,128)}, u32[]{:S(2)}) copy-start(f32[5,256,256]{2,1,0:T(8,128)} %state_ref.1) | copy-start | bytes 3932164
  7.7 1.2 %copy-start.3 = (f32[5,32768]{1,0:T(8,128)S(1)}, f32[5,32768]{1,0:T(8,128)}, u32[]{:S(2)}) copy-start(f32[5,32768]{1,0:T(8,128)} %src_ref.1) | copy-start | bytes 1966084
  9.0 0.9 copy-start.4
  9.9 0.7 copy-start.5
  14.7 1.0 copy-start.2
  15.7 5.3 %copy-start.8 = (f32[256,256]{1,0:T(8,128)S(1)}, f32[256,256]{1,0:T(8,128)}, u32[]{:S(2)}) copy-start(f32[256,256]{1,0:T(8,128)} %param.9) | copy-start | bytes 786436
  15.7 6.0 %copy-start.11 = (s32[8]{0:T(128)S(1)}, s32[8]{0:T(128)}, u32[]{:S(2)}) copy-start(s32[8]{0:T(128)} %param.13) | copy-start | bytes 100
  15.7 7.9 %copy-start.10 = (s32[8]{0:T(128)S(1)}, s32[8]{0:T(128)}, u32[]{:S(2)}) copy-start(s32[8]{0:T(128)} %param.14) | copy-start | bytes 100
  15.7 9.2 %copy-start.1 = (f32[5,256,256]{2,1,0:T(8,128)S(1)}, f32[5,256,256]{2,1,0:T(8,128)}, u32[]{:S(2)}) copy-start(f32[5,256,256]{2,1,0:T(8,128)} %state_ref.1) | copy-start | bytes 3932164
  15.7 25.8 %all-to-all-start = ((f32[8,288,128]{2,1,0:T(8,128)}), f32[8,288,128]{2,1,0:T(8,128)S(1)}, u32[]{:S(2)}, u32[]{:S(2)}) async-start(f32[8,288,128]{2,1,0:T(8,128)} %bitcast.16), calls=%async_computation | async-start | bytes 2359296 | tf_op jit(solution)/shard_map/all_to_all | solution.py:277
  27.8 8.8 %collective-permute-start.3 = (f32[5,258,1]{1,2,0:T(1,128)S(1)}, f32[5,258,1]{1,2,0:T(1,128)S(1)}, u32[]{:S(2)}, u32[]{:S(2)}) collective-permute-start(f32[5,258,1]{1,2,0:T(1,128)S(1)} %copy.11), channel_id=1, source_target_pairs={{0,1},{1,2},{2,3},{4,5},{5,6},{6,7},{8,9},{9,10},{10,11},{12,13},{... | collective-permute-start | bytes 15488 | tf_op jit(solution)/shard_map/ppermute | solution.py:31
  31.1 5.3 %collective-permute-start.2 = (f32[5,258,1]{1,2,0:T(1,128)S(1)}, f32[5,258,1]{1,2,0:T(1,128)S(1)}, u32[]{:S(2)}, u32[]{:S(2)}) collective-permute-start(f32[5,258,1]{1,2,0:T(1,128)S(1)} %copy.9), channel_id=1, source_target_pairs={{1,0},{2,1},{3,2},{5,4},{6,5},{7,6},{9,8},{10,9},{11,10},{13,12},{... | collective-permute-start | bytes 15488 | tf_op jit(solution)/shard_map/ppermute | solution.py:33
  65.4 4.8 %collective-permute-start.4 = (f32[5,4,256]{2,1,0:T(4,128)S(1)}, f32[5,4,256]{2,1,0:T(4,128)S(1)}, u32[]{:S(2)}, u32[]{:S(2)}) collective-permute-start(f32[5,4,256]{2,1,0:T(4,128)S(1)} %get-tuple-element.13), channel_id=1, source_target_pairs={{0,4},{4,8},{8,12},{12,16},{16,20},{20,24},{24,28},{1,5},{5,9},{9,... | collective-permute-start | bytes 61448 | tf_op jit(solution)/shard_map/ppermute | solution.py:31
  67.8 6.0 %collective-permute-start.5 = (f32[5,4,256]{2,1,0:T(4,128)S(1)}, f32[5,4,256]{2,1,0:T(4,128)S(1)}, u32[]{:S(2)}, u32[]{:S(2)}) collective-permute-start(f32[5,4,256]{2,1,0:T(4,128)S(1)} %get-tuple-element.14), channel_id=1, source_target_pairs={{4,0},{8,4},{12,8},{16,12},{20,16},{24,20},{28,24},{5,1},{9,5},{13... | collective-permute-start | bytes 61448 | tf_op jit(solution)/shard_map/ppermute | solution.py:33
  81.1 1.5 %copy-start.7 = (f32[5,256,256]{2,1,0:T(8,128)}, f32[5,256,256]{2,1,0:T(8,128)S(1)}, u32[]{:S(2)}) copy-start(f32[5,256,256]{2,1,0:T(8,128)S(1)} %fusion.26) | copy-start | bytes 3932164
  82.6 8.5 %copy-start.9 = (f32[4]{0:T(128)S(1)}, f32[4]{0:T(128)}, u32[]{:S(2)}) copy-start(f32[4]{0:T(128)} %constant.32.clone) | copy-start | bytes 52
  82.6 13.7 %copy-start.6 = (f32[5,258,257]{2,1,0:T(8,128)S(1)}, f32[5,258,257]{2,1,0:T(8,128)}, u32[]{:S(2)}) copy-start(f32[5,258,257]{2,1,0:T(8,128)} %get-tuple-element.7) | copy-start | bytes 3978364
  85.4 9.7 %collective-permute-start.7 = (f32[5,256,4]{1,2,0:T(4,128)S(1)}, f32[5,256,4]{1,2,0:T(4,128)S(1)}, u32[]{:S(2)}, u32[]{:S(2)}) collective-permute-start(f32[5,256,4]{1,2,0:T(4,128)S(1)} %copy.15), channel_id=1, source_target_pairs={{1,0},{2,1},{3,2},{5,4},{6,5},{7,6},{9,8},{10,9},{11,10},{13,12},{... | collective-permute-start | bytes 61448 | tf_op jit(solution)/shard_map/ppermute | solution.py:33
  89.2 4.9 %collective-permute-start.6 = (f32[5,256,4]{1,2,0:T(4,128)S(1)}, f32[5,256,4]{1,2,0:T(4,128)S(1)}, u32[]{:S(2)}, u32[]{:S(2)}) collective-permute-start(f32[5,256,4]{1,2,0:T(4,128)S(1)} %copy.13), channel_id=1, source_target_pairs={{0,1},{1,2},{2,3},{4,5},{5,6},{6,7},{8,9},{9,10},{10,11},{12,13},{... | collective-permute-start | bytes 61448 | tf_op jit(solution)/shard_map/ppermute | solution.py:31

commit v3 on v2

--- a/solution.py
+++ b/solution.py
@@ -2,6 +2,7 @@
 
 import jax
 import jax.numpy as jnp
+import numpy as np
 from jax import lax
 from jax.experimental import pallas as pl
 from jax.experimental.pallas import tpu as pltpu
@@ -13,53 +14,66 @@
 WINDOW = 64
 ROUNDS = 2
 UNROLL = 8
-WIDE = False
 STEP = 4
 
 time_step = 0.25
 layer_weights = (1.0, 0.6, 0.35, 0.2)
 
 
-def extended(cells, sides, width):
-    for axis, dim in sides:
-        count = lax.axis_size(axis)
-        ends = count - 1
-        head = lax.slice_in_dim(cells, 0, width, axis=dim)
-        tail = lax.slice_in_dim(cells, cells.shape[dim] - width, cells.shape[dim], axis=dim)
-        cells = jnp.concatenate(
-            [
-                lax.ppermute(tail, axis, [(i, (i + 1) % count) for i in range(ends)]),
-                cells,
-                lax.ppermute(head, axis, [((i + 1) % count, i) for i in range(ends)]),
-            ],
-            axis=dim,
-        )
-    return cells
-
-
 def filter_weights(half_width):
-    offsets = jnp.arange(-half_width, half_width + 1).astype(jnp.float32)
-    bell_curve = jnp.exp(-offsets * offsets / 8.0)
-    return bell_curve / jnp.sum(bell_curve)
-
-
-def smooth_axis(padded, half_width, axis_dim, length):
-    weights = filter_weights(half_width)
-    summed = weights[0] * lax.slice_in_dim(padded, 0, length, axis=axis_dim)
-    for tap_index in range(1, 2 * half_width + 1):
-        summed = summed + weights[tap_index] * lax.slice_in_dim(
-            padded, tap_index, tap_index + length, axis=axis_dim
-        )
-    return summed
-
-
-def laplace_nine(padded):
-    centre = padded[:, 1:-1, 1:-1]
-    edge_sum = (
-        padded[:, 2:, 1:-1] + padded[:, :-2, 1:-1] + padded[:, 1:-1, 2:] + padded[:, 1:-1, :-2]
-    )
-    corners = padded[:, 2:, 2:] + padded[:, 2:, :-2] + padded[:, :-2, 2:] + padded[:, :-2, :-2]
-    return (4.0 * edge_sum + corners - 20.0 * centre) / 6.0
+    offsets = np.arange(-half_width, half_width + 1).astype(np.float32)
+    bell_curve = np.exp(-offsets * offsets / np.float32(8.0))
+    return bell_curve / np.sum(bell_curve)
+
+
+def taps(targets, length):
+    weights = filter_weights(FW)
+    table = np.zeros((len(targets), length), np.float32)
+    for i, cell in enumerate(targets):
+        if cell is not None:
+            for k in range(-FW, FW + 1):
+                if 0 <= cell + k < length:
+                    table[i, cell + k] = weights[k + FW]
+    return table
+
+
+def edge_targets(length):
+    gap = [None] * (8 - FW)
+    return list(range(-FW, 0)) + gap + list(range(length, length + FW)) + gap
+
+
+def extended_targets(length):
+    gap = [None] * (LANES - FW)
+    return list(range(length)) + gap + list(range(-FW, 0)) + list(range(length, length + FW)) + gap
+
+
+def pick_columns(radial):
+    table = np.zeros((16, 2 * radial), np.float32)
+    for k in range(FW):
+        table[k, k] = 1.0
+        table[8 + k, radial - FW + k] = 1.0
+    table[FW, radial] = 1.0
+    table[8 + FW, 2 * radial - 1] = 1.0
+    return table
+
+
+def halves(x):
+    high = x.astype(jnp.bfloat16)
+    return high, (x - high.astype(jnp.float32)).astype(jnp.bfloat16)
+
+
+def product(x, y, dims):
+    xh, xl = halves(x) if not isinstance(x, tuple) else x
+    yh, yl = halves(y) if not isinstance(y, tuple) else y
+
+    def dot(p, q):
+        return lax.dot_general(p, q, (dims, ((), ())), preferred_element_type=jnp.float32)
+
+    return dot(xh, yh) + (dot(xl, yh) + dot(xh, yl))
+
+
+PLAIN = ((1,), (0,))
+TURNED = ((1,), (1,))
 
 
 def comparators(count):
@@ -88,12 +102,11 @@
     return tiles
 
 
-def pack_kernel(cap_tiles, step, base, count_ref, src_ref, cell_ref, state_ref, out_ref, held_ref):
+def pack_kernel(cap_tiles, step, base, azim, count_ref, src_ref, cell_ref, face_ref, out_ref, held_ref):
     components = src_ref.shape[0]
     fields = components + 1
     tile_count = cell_ref.shape[0]
-    radial = state_ref.shape[2]
-    azim = state_ref.shape[1]
+    radial = face_ref.shape[2]
     slot_rows = base + 8 + -(-fields * cap_tiles // 8) * 8
     seg_count = out_ref.shape[0] // slot_rows
     lane = lax.broadcasted_iota(jnp.int32, (8, LANES), 1)
@@ -116,7 +129,7 @@
         row = g * slot_rows
         for v in range(components):
             for half in range(2):
-                out_ref[pl.ds(row + 8 * v + 4 * half, JL), :] = state_ref[
+                out_ref[pl.ds(row + 8 * v + 4 * half, JL), :] = face_ref[
                     v, 0:JL, half * LANES : (half + 1) * LANES
                 ]
         head = rolled(0)
@@ -160,10 +173,56 @@
     lax.fori_loop(0, seg_count // 8, group, 0)
 
 
-def deposit_kernel(cap_tiles, base, step, got_ref, out_ref, bound_ref, sum_ref, limit_ref, work_ref, sem):
+def base_kernel(state_ref, kappa_ref, out_ref, edge_ref):
+    components, azim, radial = state_ref.shape
+    lane = lax.broadcasted_iota(jnp.int32, (azim, radial), 1)
+    sub = lax.broadcasted_iota(jnp.int32, (8, radial), 0)
+    first = lane[:1] == 0
+    last = lane[:1] == radial - 1
+    pick = lax.broadcasted_iota(jnp.int32, (8, radial), 1)
+    pick = ((sub == 2) & (pick == 0)) | ((sub == 3) & (pick == radial - 1))
+    pick = jnp.where(pick, 1.0, 0.0).astype(jnp.bfloat16)
+    none = jnp.zeros((1, radial), jnp.float32)
+
+    def component(v, carry):
+        q = state_ref[v]
+        both = jnp.concatenate([q[1:], none], axis=0) + jnp.concatenate([none, q[:-1]], axis=0)
+        column = both + 4.0 * q
+        side = jnp.where(lane == radial - 1, 0.0, pltpu.roll(column, radial - 1, 1)) + jnp.where(
+            lane == 0, 0.0, pltpu.roll(column, 1, 1)
+        )
+        total = side + (4.0 * both - 20.0 * q)
+        out_ref[v] = q + time_step * (kappa_ref[...] * total / 6.0)
+
+        def along(row):
+            right = jnp.where(last, 0.0, pltpu.roll(row, radial - 1, 1))
+            left = jnp.where(first, 0.0, pltpu.roll(row, 1, 1))
+            return 4.0 * row + right + left
+
+        top, bottom = q[:1], q[-1:]
+        high, low = halves(column)
+        turned = sum(
+            lax.dot_general(pick, x, (TURNED, ((), ())), preferred_element_type=jnp.float32) for x in (high, low)
+        )
+        edge_ref[v] = jnp.where(
+            sub == 0,
+            along(top),
+            jnp.where(sub == 1, along(bottom), jnp.where(sub == 4, top, jnp.where(sub == 5, bottom, turned))),
+        )
+        return carry
+
+    lax.fori_loop(0, components, component, 0)
+
+
+def deposit_kernel(
+    cap_tiles, base, step,
+    map_ref, match_ref, got_ref, face_ref, edge_ref, near_ref, far_ref,
+    sum_ref, joint_ref, before_ref, after_ref, side_ref,
+    bound_ref, limit_ref, work_ref, sem,
+):
     seg_count, slot_rows, _ = got_ref.shape
-    components = out_ref.shape[0]
-    azim, radial = out_ref.shape[1:]
+    components, _, radial = sum_ref.shape
+    azim = sum_ref.shape[1] - WINDOW
     fields = components + 1
     width = step * LANES
     chunk_count = cap_tiles // step
@@ -204,7 +263,7 @@
         work_ref[1, total + u] = 0
         work_ref[2, total + u] = azim
 
-    def product(t):
+    def block(t):
         s = work_ref[0, t]
         begin = work_ref[1, t]
         start = pl.multiple_of(work_ref[2, t], 8)
@@ -227,32 +286,160 @@
             low = (values - high.astype(jnp.float32)).astype(jnp.bfloat16)
             highs.append(jnp.where(in_a, high, jnp.bfloat16(0)))
             lows.append(jnp.where(in_a, low, jnp.bfloat16(0)))
-        if WIDE:
-            left = jnp.concatenate([jnp.concatenate(highs, axis=0), jnp.concatenate(lows, axis=0)], axis=1)
-            part = lax.dot_general(
-                left, jnp.concatenate([right, right], axis=1), (((1,), (1,)), ((), ())), preferred_element_type=jnp.float32
-            )
-        else:
-            left = jnp.concatenate(highs + lows, axis=0)
-            part = lax.dot_general(
-                left, right, (((1,), (1,)), ((), ())), preferred_element_type=jnp.float32
-            )
-            part = part[: components * WINDOW] + part[components * WINDOW :]
+        left = jnp.concatenate(highs + lows, axis=0)
+        part = lax.dot_general(left, right, (TURNED, ((), ())), preferred_element_type=jnp.float32)
+        part = part[: components * WINDOW] + part[components * WINDOW :]
         return start, part
 
     def several(t, carry):
-        done = [product(t * UNROLL + u) for u in range(UNROLL)]
+        done = [block(t * UNROLL + u) for u in range(UNROLL)]
         for start, part in done:
             for v in range(components):
                 sum_ref[v, pl.ds(start, WINDOW), :] += part[v * WINDOW : (v + 1) * WINDOW]
         return carry
 
     lax.fori_loop(0, (total + UNROLL - 1) // UNROLL, several, 0)
-    out_ref[...] = sum_ref[:, :azim, :]
+
+    own = lax.axis_index("segaz")
+    partner = jnp.int32(0)
+    target = match_ref[map_ref[own]]
+    for h in range(seg_count):
+        partner = jnp.where(map_ref[h] == target, h, partner)
+    layer = lax.broadcasted_iota(jnp.int32, (JL, radial), 0)
+    strength = jnp.zeros((JL, radial), jnp.float32)
+    for l in range(JL):
+        strength = jnp.where(layer == l, layer_weights[l], strength)
+    for v in range(components):
+        tile = got_ref[partner, 8 * v : 8 * v + 8, :]
+        face = jnp.concatenate([tile[:JL], tile[JL:]], axis=1)
+        joint_ref[v, 0:JL, :] = strength * (face - face_ref[v, 0:JL, :])
+        joint_ref[v, JL:8, :] = jnp.zeros((8 - JL, radial), jnp.float32)
+
+    near = halves(near_ref[...])
+    far = halves(far_ref[...])
+    inner = tuple(x[:, :radial] for x in far)
+    rows, columns = [], []
+    for v in range(components):
+        cells_v = halves(sum_ref[v, 0:azim, :])
+        rows.append(product(near, cells_v, PLAIN))
+        columns.append(product(near, cells_v, TURNED))
+    rows = product(jnp.concatenate(rows, axis=0), inner, PLAIN)
+    columns = product(jnp.concatenate(columns, axis=0), far, PLAIN)
+    sub = lax.broadcasted_iota(jnp.int32, (8, LANES), 0)
+    lane = lax.broadcasted_iota(jnp.int32, (8, LANES), 1)
+    half = LANES
+    for v in range(components):
+        row = rows[16 * v : 16 * v + 16]
+        column = columns[16 * v : 16 * v + 16]
+        edge = edge_ref[v]
+        wide = lax.broadcasted_iota(jnp.int32, (8, radial), 0)
+        after_ref[v, :, :radial] = jnp.where(wide == FW, edge[1:2], row[8:16])
+        before_ref[v, :, :radial] = jnp.where(
+            wide == FW - 1, edge[0:1], jnp.concatenate([row[FW:8], row[0:FW]], axis=0)
+        )
+        bottom, top = edge[5:6], edge[4:5]
+        left_corner = jnp.where(lane[:1] == 0, bottom[:, :half], 0.0)
+        right_corner = jnp.where(lane[:1] == 0, pltpu.roll(bottom[:, radial - half :], 1, 1), 0.0)
+        after_ref[v, :, radial : radial + half] = jnp.where(
+            sub == FW, left_corner, column[0:8, radial + half : radial + 2 * half]
+        )
+        after_ref[v, :, radial + half : radial + 2 * half] = jnp.where(
+            sub == FW, right_corner, column[8:16, radial + half : radial + 2 * half]
+        )
+        left_corner = jnp.where(lane[:1] == half - 1, pltpu.roll(top[:, :half], half - 1, 1), 0.0)
+        right_corner = jnp.where(lane[:1] == half - 1, top[:, radial - half :], 0.0)
+        before_ref[v, :, radial : radial + half] = jnp.where(
+            sub == FW, left_corner, column[0:8, radial : radial + half]
+        )
+        before_ref[v, :, radial + half : radial + 2 * half] = jnp.where(
+            sub == FW, right_corner, column[8:16, radial : radial + half]
+        )
+        side_ref[v, 0:8, :] = jnp.where(wide == FW, edge[2:3], column[0:8, :radial])
+        side_ref[v, 8:16, :] = jnp.where(wide == FW, edge[3:4], column[8:16, :radial])
+
+
+def inner_kernel(sum_ref, base_ref, joint_ref, band_ref, out_ref):
+    components, azim, radial = base_ref.shape
+    band = halves(band_ref[...])
+
+    def component(v, carry):
+        across = product(sum_ref[v, 0:azim, :], band, PLAIN)
+        both = product(band, across, PLAIN)
+        out_ref[v] = base_ref[v] + time_step * both
+        out_ref[v, 0:8, :] += time_step * joint_ref[v]
+        return carry
+
+    lax.fori_loop(0, components, component, 0)
+
+
+def corner_kernel(side_ref, prior_ref, next_ref, left_ref, right_ref):
+    radial = left_ref.shape[2]
+    for out_ref, begin, corner in ((left_ref, 0, radial), (right_ref, 8, radial + LANES)):
+        out_ref[:, :, :LANES] = (
+            side_ref[:, begin : begin + 8, :LANES] + prior_ref[:, :, corner : corner + LANES]
+        )
+        out_ref[:, :, LANES:] = (
+            side_ref[:, begin : begin + 8, LANES:] + next_ref[:, :, corner : corner + LANES]
+        )
+
+
+def final_kernel(inner_ref, kappa_ref, prior_ref, next_ref, left_ref, right_ref, pick_ref, out_ref):
+    components, azim, radial = inner_ref.shape
+    pick = pick_ref[...].astype(jnp.bfloat16)
+    sub = lax.broadcasted_iota(jnp.int32, (8, radial), 0)
+
+    def component(v, carry):
+        parts = halves(jnp.concatenate([left_ref[v], right_ref[v]], axis=0))
+        sides = sum(
+            lax.dot_general(x, pick, (((0,), (0,)), ((), ())), preferred_element_type=jnp.float32) for x in parts
+        )
+        kappa = kappa_ref[...]
+        out_ref[v] = inner_ref[v] + time_step * (sides[:, :radial] + kappa * sides[:, radial:] / 6.0)
+        prior = prior_ref[v, :, :radial]
+        add = jnp.where(sub < FW, prior, 0.0) + jnp.where(
+            sub == 0, kappa[0:8] * prior[FW : FW + 1] / 6.0, 0.0
+        )
+        out_ref[v, 0:8, :] += time_step * add
+        nxt = next_ref[v, :, :radial]
+        add = jnp.where(sub >= 8 - FW, nxt, 0.0) + jnp.where(
+            sub == 7, kappa[azim - 8 : azim] * nxt[FW - 1 : FW] / 6.0, 0.0
+        )
+        out_ref[v, azim - 8 : azim, :] += time_step * add
+        return carry
+
+    lax.fori_loop(0, components, component, 0)
+
+
+def call(kernel, outs, ins, scratch=(), cost=None):
+    def spec(where):
+        if where == "smem":
+            return pl.BlockSpec(memory_space=pltpu.SMEM)
+        if where == "vmem":
+            return pl.BlockSpec(memory_space=pltpu.VMEM)
+        return pl.BlockSpec(where, lambda i: (0,) * len(where))
+
+    return pl.pallas_call(
+        kernel,
+        grid=(1,),
+        out_shape=[jax.ShapeDtypeStruct(shape, jnp.float32) for shape in outs],
+        in_specs=[spec(where) for where in ins],
+        out_specs=[pl.BlockSpec(memory_space=pltpu.VMEM)] * len(outs),
+        scratch_shapes=list(scratch),
+        cost_estimate=None
+        if cost is None
+        else pl.CostEstimate(flops=cost, bytes_accessed=cost // 1000, transcendentals=0),
+        compiler_params=pltpu.CompilerParams(vmem_limit_bytes=48 << 20),
+    )
+
+
+def shifted(strip, axis, way):
+    count = lax.axis_size(axis)
+    pairs = [(i, i + 1) if way > 0 else (i + 1, i) for i in range(count - 1)]
+    return lax.ppermute(strip, axis, pairs)
 
 
 def local(state, kappa, drop_src, drop_cell, drop_count, part_map, match_block):
-    components, azim_cells, radial_cells = state.shape
+    components, azim, radial = state.shape
     row_count = drop_src.shape[1]
     seg_count = lax.axis_size("segaz")
     capacity = 5 * row_count // (4 * seg_count)
@@ -261,53 +448,44 @@
     base = 8 * components
     fields = components + 1
     slot_rows = base + 8 + -(-fields * cap_tiles // 8) * 8
-    own_index = lax.axis_index("segaz")
-    indices = jnp.arange(seg_count, dtype=jnp.int32)
-    vmem = pl.BlockSpec(memory_space=pltpu.VMEM)
-    smem = pl.BlockSpec(memory_space=pltpu.SMEM)
-    sends = pl.pallas_call(
-        functools.partial(pack_kernel, cap_tiles, step, base),
-        out_shape=jax.ShapeDtypeStruct((seg_count * slot_rows, LANES), jnp.float32),
-        in_specs=[smem, vmem, vmem, vmem],
-        out_specs=vmem,
-        scratch_shapes=[pltpu.VMEM((seg_count // 8, cap_tiles, 64, LANES), jnp.float32)],
-        compiler_params=pltpu.CompilerParams(vmem_limit_bytes=48 << 20),
+    items = seg_count * (cap_tiles // step) * (azim // WINDOW + 2) + UNROLL
+    face = (components, 8, radial)
+    whole = state.shape
+    strip = (components, 8, 2 * radial)
+    sides = (components, 8, radial)
+    (sends,) = call(
+        functools.partial(pack_kernel, cap_tiles, step, base, azim),
+        [(seg_count * slot_rows, LANES)],
+        ["smem", "vmem", "vmem", face],
+        [pltpu.VMEM((seg_count // 8, cap_tiles, 64, LANES), jnp.float32)],
     )(drop_count, drop_src, drop_cell.reshape(-1, LANES), state)
-    sends = sends.reshape(seg_count, slot_rows, LANES)
-    got = lax.all_to_all(sends, "segaz", split_axis=0, concat_axis=0, tiled=True)
-    source = pl.pallas_call(
+    got = lax.all_to_all(
+        sends.reshape(seg_count, slot_rows, LANES), "segaz", split_axis=0, concat_axis=0, tiled=True
+    )
+    still, edge = call(base_kernel, [whole, face], ["vmem", "vmem"], cost=1 << 22)(state, kappa)
+    near = jnp.asarray(taps(edge_targets(azim), azim))
+    far = jnp.asarray(taps(extended_targets(azim), azim).T)
+    band = jnp.asarray(taps(list(range(azim)), azim))
+    source, joint, before, after, side = call(
         functools.partial(deposit_kernel, cap_tiles, base, step),
-        out_shape=jax.ShapeDtypeStruct(state.shape, jnp.float32),
-        in_specs=[vmem],
-        out_specs=vmem,
-        scratch_shapes=[
+        [(components, azim + WINDOW, radial), face, strip, strip, (components, 16, radial)],
+        ["smem", "smem", "vmem", face, "vmem", "vmem", "vmem"],
+        [
             pltpu.VMEM((seg_count, LANES), jnp.int32),
-            pltpu.VMEM((components, azim_cells + WINDOW, radial_cells), jnp.float32),
             pltpu.SMEM((seg_count, LANES), jnp.int32),
-            pltpu.SMEM((3, seg_count * (cap_tiles // step) * (azim_cells // WINDOW + 2) + UNROLL), jnp.int32),
+            pltpu.SMEM((3, items), jnp.int32),
             pltpu.SemaphoreType.DMA(()),
         ],
-        compiler_params=pltpu.CompilerParams(vmem_limit_bytes=48 << 20),
-    )(got)
-
-    padded = extended(state, (("segaz", 1), ("rad", 2)), 1)
-    diffusion = kappa[None] * laplace_nine(padded)
-    my_block = jnp.sum(jnp.where(indices == own_index, part_map, 0))
-    target = jnp.sum(jnp.where(indices == my_block, match_block, 0))
-    partner = jnp.sum(jnp.where(part_map == target, indices, 0))
-    face_rows = state[:, :JL, :]
-    partner_face = lax.dynamic_index_in_dim(got, partner, 0, keepdims=False)[:base]
-    partner_face = partner_face.reshape(components, 2, JL, LANES).transpose(0, 2, 1, 3).reshape(face_rows.shape)
-    weights = jnp.array(layer_weights, jnp.float32)
-    coupling = weights[None, :, None] * (partner_face - face_rows)
-    junction = jnp.concatenate(
-        [coupling, jnp.zeros((components, azim_cells - JL, radial_cells), jnp.float32)], axis=1
-    )
-    wide_azim = extended(source, (("segaz", 1),), FW)
-    smoothed = smooth_axis(wide_azim, FW, 1, azim_cells)
-    wide_radial = extended(smoothed, (("rad", 2),), FW)
-    filtered = smooth_axis(wide_radial, FW, 2, radial_cells)
-    return state + time_step * (diffusion + junction + filtered)
+    )(part_map, match_block, got, state, edge, near, far)
+    prior = shifted(after, "segaz", 1)
+    nxt = shifted(before, "segaz", -1)
+    (inner,) = call(inner_kernel, [whole], ["vmem"] * 4, cost=1 << 22)(source, still, joint, band)
+    to_left, to_right = call(corner_kernel, [sides, sides], ["vmem"] * 3)(side, prior, nxt)
+    left = shifted(to_right, "rad", 1)
+    right = shifted(to_left, "rad", -1)
+    pick = jnp.asarray(pick_columns(radial))
+    (result,) = call(final_kernel, [whole], ["vmem"] * 7)(inner, kappa, prior, nxt, left, right, pick)
+    return result
 
 
 def solution(mesh):

time: 115 us -> 76.7 us (0.67)
  other arithmetic: 33.9 us -> 0 us
  local copies, waits for them, and re-layouts: 17.3 us -> 6.23 us
  waiting for transfers between devices: 6.49 us -> 17.5 us
  starting transfers between devices: 26 us -> 16.9 us
  Pallas kernels: 28 us -> 35.4 us
  between operations: 2.12 us -> 0.21 us
    add x2 -> x0, other arithmetic: 24.9 us -> none  [the longest x1 17.6 us: local(): return state + time_step * (diffusion + junction + filtered)]
    all_to_all x1, waiting for transfers between devices: 0.01 us -> 12.8 us  [local(): lax.all_to_all(sends.reshape(seg_count, slot_rows, LANES), 'segaz', split...]
    ppermute x8 -> x4, starting transfers between devices: 21.3 us -> 12.2 us  [shifted(): return lax.ppermute(strip, axis, pairs)]
    slice x10 -> x0, local copies, waits for them, and re-layouts: 8.48 us -> none  [the longest x5 4.02 us: extended(): lax.slice_in_dim(cells, cells.shape[dim] - width, cells.shape[dim], axis=...]
    pallas_call x2 -> x6, Pallas kernels: 28 us -> 35.4 us  [the longest x1 23.8 us: local(): call(functools.partial(deposit_kernel, cap_tiles, base, step), [(componen...]
    reduce_sum x4 -> x0, other arithmetic: 3.82 us -> none  [the longest x1 1.29 us: local(): target = jnp.sum(jnp.where(indices == my_block, match_block, 0))]
    concatenate x2 -> x0, other arithmetic: 3.82 us -> none  [extended(): jnp.concatenate([lax.ppermute(tail, axis, [(i, (i + 1) % count) for i in...]
    ppermute x4 -> x0, local copies, waits for them, and re-layouts: 3.64 us -> none  [the longest x2 2.25 us: extended(): lax.ppermute(tail, axis, [(i, (i + 1) % count) for i in range(ends)])]
  transfers between devices with their start and end apart: 9 -> 5, of which waited for: 2 -> 2; matrix products, arithmetic and copies ran while one was open for 13% -> 0% of each run, Pallas kernels for 4% -> 6%
where the time goes in v3:
time: 76.7 us; the launch traced here: 76.2 us
  Pallas kernels  35.4 us (46%)
  waiting for transfers between devices  17.5 us (23%)
  starting transfers between devices  16.9 us (22%)
  local copies, waits for them, and re-layouts  6.23 us (8%)
    pallas_call x1, Pallas kernels, local(): call(functools.partial(deposit_kernel, cap_tiles, base, step), [(componen...  23.8 us
    all_to_all x1, waiting for transfers between devices, local(): lax.all_to_all(sends.reshape(seg_count, slot_rows, LANES), 'segaz', split...  12.8 us
    ppermute x4, starting transfers between devices, shifted(): return lax.ppermute(strip, axis, pairs)  12.2 us
    unnamed x30, local copies, waits for them, and re-layouts  6.23 us
    ppermute x4, waiting for transfers between devices, shifted(): return lax.ppermute(strip, axis, pairs)  4.73 us
    all_to_all x1, starting transfers between devices, local(): lax.all_to_all(sends.reshape(seg_count, slot_rows, LANES), 'segaz', split...  4.7 us
    pallas_call x1, Pallas kernels, local(): call(functools.partial(pack_kernel, cap_tiles, step, base, azim), [(seg_c...  4.14 us
    pallas_call x1, Pallas kernels, local(): call(inner_kernel, [whole], ['vmem'] * 4, cost=1 << 22)  3.45 us
  transfers between devices with their start and end apart: 5, of which 2 were waited for; matrix products, arithmetic and copies ran while one was open for 0% of the time, Pallas kernels for 6%

profile of v3, /device:TPU:19, one launch (start us, length us, event | category | flops | bytes accessed | tf_op | source)
XLA Modules:
  0.0 76.2 jit_solution(4691452643977404898)
XLA Ops:
  0.0 0.0 copy-start
  0.0 1.3 %copy-done = f32[5,256,256]{2,1,0:T(8,128)S(1)} copy-done((f32[5,256,256]{2,1,0:T(8,128)S(1)}, f32[5,256,256]{2,1,0:T(8,128)}, u32[]{:S(2)}) %copy-start) | copy-done | bytes 1310744
  1.3 0.0 copy-start.6
  1.3 1.2 %copy-done.6 = f32[5,32768]{1,0:T(8,128)S(1)} copy-done((f32[5,32768]{1,0:T(8,128)S(1)}, f32[5,32768]{1,0:T(8,128)}, u32[]{:S(2)}) %copy-start.6) | copy-done | bytes 655384
  2.5 0.0 copy-start.9
  2.5 0.9 %copy-done.9 = s32[32768]{0:T(1024)S(1)} copy-done((s32[32768]{0:T(1024)S(1)}, s32[32768]{0:T(1024)}, u32[]{:S(2)}) %copy-start.9) | copy-done | bytes 131096
  3.4 0.0 copy-start.14
  3.4 0.7 copy-done.14
  4.1 4.1 %shard_map.109 = f32[2304,128]{1,0:T(8,128)S(1)} custom-call(s32[1,8]{1,0:T(1,128)S(1)} %copy-done.14, f32[5,32768]{1,0:T(8,128)S(1)} %copy-done.6, s32[256,128]{1,0:T(8,128)S(1)} %bitcast.3, f32[5,256,256]{2,1,0:T(8,128)S(1)} %copy-done), custom_call_target="tpu_custom_call" | custom-call | tf_op jit(solution)/shard_map/pallas_call | solution.py:456
  8.2 0.0 copy-start.2
  8.3 1.0 %copy-done.2 = f32[2304,128]{1,0:T(8,128)} copy-done((f32[2304,128]{1,0:T(8,128)}, f32[2304,128]{1,0:T(8,128)S(1)}, u32[]{:S(2)}) %copy-start.2) | copy-done | bytes 1179672
  9.3 0.0 copy-start.1
  9.3 0.0 copy-start.5
  9.3 4.7 %all-to-all-start = ((f32[8,288,128]{2,1,0:T(8,128)}), f32[8,288,128]{2,1,0:T(8,128)S(1)}, u32[]{:S(2)}, u32[]{:S(2)}) async-start(f32[8,288,128]{2,1,0:T(8,128)} %bitcast.2), calls=%async_computation | async-start | bytes 2359296 | tf_op jit(solution)/shard_map/all_to_all | solution.py:462
  14.0 0.0 copy-done.1
  14.0 0.0 copy-done.5
  14.0 0.0 copy-start.7
  14.0 0.0 copy-start.11
  14.0 0.0 copy-start.12
  14.0 0.0 copy-start.13
  14.0 1.3 %shard_map.110 = (f32[5,256,256]{2,1,0:T(8,128)S(1)}, f32[5,8,256]{2,1,0:T(8,128)S(1)}) custom-call(f32[5,256,256]{2,1,0:T(8,128)S(1)} %copy-done.1, f32[256,256]{1,0:T(8,128)S(1)} %copy-done.5), custom_call_target="tpu_custom_call" | custom-call | flops 4194304 | bytes 4194 | tf_op jit(solution)/shard_map/pallas_call | solution.py:465
  15.4 0.0 copy-start.3
  15.4 1.0 %copy-done.3 = f32[5,256,256]{2,1,0:T(8,128)} copy-done((f32[5,256,256]{2,1,0:T(8,128)}, f32[5,256,256]{2,1,0:T(8,128)S(1)}, u32[]{:S(2)}) %copy-start.3) | copy-done | bytes 1310744
  16.4 12.8 %all-to-all-done.got_ref = f32[8,288,128]{2,1,0:T(8,128)S(1)} async-done(((f32[8,288,128]{2,1,0:T(8,128)}), f32[8,288,128]{2,1,0:T(8,128)S(1)}, u32[]{:S(2)}, u32[]{:S(2)}) %all-to-all-start) | async-done | bytes 1179680 | tf_op jit(solution)/shard_map/all_to_all | solution.py:462
  29.2 0.0 copy-done.7
  29.2 0.0 copy-done.11
  29.2 0.0 copy-done.12
  29.2 0.0 copy-done.13
  29.2 0.0 copy-start.4
  29.2 0.0 copy-start.8
  29.3 23.8 %shard_map.111 = (f32[5,320,256]{2,1,0:T(8,128)S(1)}, f32[5,8,256]{2,1,0:T(8,128)S(1)}, f32[5,8,512]{2,1,0:T(8,128)S(1)}, f32[5,8,512]{2,1,0:T(8,128)S(1)}, f32[5,16,256]{2,1,0:T(8,128)S(1)}) custom-call(s32[8]{0:T(128)S(1)} %copy-done.12, s32[8]{0:T(128)S(1)} %copy-done.13, f32[8,288,128]{2,1,0:T(8,128)S(1)} %all-to-all-done.got_ref, ...), custom_call_target="tpu_custom_call" | custom-call | tf_op jit(solution)/shard_map/pallas_call | solution.py:469
  53.0 3.4 %collective-permute-start = (f32[5,8,512]{2,1,0:T(8,128)S(1)}, f32[5,8,512]{2,1,0:T(8,128)S(1)}, u32[]{:S(2)}, u32[]{:S(2)}) collective-permute-start(f32[5,8,512]{2,1,0:T(8,128)S(1)} %get-tuple-element.18), channel_id=1, source_target_pairs={{0,4},{4,8},{8,12},{12,16},{16,20},{20,24},{24,28},{1,5},{5,9},{9,... | collective-permute-start | bytes 245768 | tf_op jit(solution)/shard_map/ppermute | solution.py:438
  56.5 1.9 %collective-permute-start.1 = (f32[5,8,512]{2,1,0:T(8,128)S(1)}, f32[5,8,512]{2,1,0:T(8,128)S(1)}, u32[]{:S(2)}, u32[]{:S(2)}) collective-permute-start(f32[5,8,512]{2,1,0:T(8,128)S(1)} %get-tuple-element.19), channel_id=1, source_target_pairs={{4,0},{8,4},{12,8},{16,12},{20,16},{24,20},{28,24},{5,1},{9,5},{13... | collective-permute-start | bytes 245768 | tf_op jit(solution)/shard_map/ppermute | solution.py:438
  58.4 0.0 collective-permute-done.prior_ref
  58.4 4.7 %collective-permute-done.1.next_ref = f32[5,8,512]{2,1,0:T(8,128)S(1)} collective-permute-done((f32[5,8,512]{2,1,0:T(8,128)S(1)}, f32[5,8,512]{2,1,0:T(8,128)S(1)}, u32[]{:S(2)}, u32[]{:S(2)}) %collective-permute-start.1) | collective-permute-done | bytes 81952 | tf_op jit(solution)/shard_map/ppermute | solution.py:438
  63.1 4.9 %collective-permute-start.2 = (f32[5,8,256]{2,1,0:T(8,128)S(1)}, f32[5,8,256]{2,1,0:T(8,128)S(1)}, u32[]{:S(2)}, u32[]{:S(2)}) collective-permute-start(f32[5,8,256]{2,1,0:T(8,128)S(1)} %get-tuple-element.21), channel_id=1, source_target_pairs={{0,1},{1,2},{2,3},{4,5},{5,6},{6,7},{8,9},{9,10},{10,11},{12,13},{... | collective-permute-start | bytes 122888 | tf_op jit(solution)/shard_map/ppermute | solution.py:438
  68.1 1.9 %collective-permute-start.3 = (f32[5,8,256]{2,1,0:T(8,128)S(1)}, f32[5,8,256]{2,1,0:T(8,128)S(1)}, u32[]{:S(2)}, u32[]{:S(2)}) collective-permute-start(f32[5,8,256]{2,1,0:T(8,128)S(1)} %get-tuple-element.22), channel_id=1, source_target_pairs={{1,0},{2,1},{3,2},{5,4},{6,5},{7,6},{9,8},{10,9},{11,10},{13,12},{... | collective-permute-start | bytes 122888 | tf_op jit(solution)/shard_map/ppermute | solution.py:438
  70.0 0.0 copy-done.4
  70.0 0.0 copy-done.8
  70.0 0.0 copy-start.10
  70.0 3.4 %shard_map.112.inner_ref = f32[5,256,256]{2,1,0:T(8,128)S(1)} custom-call(f32[5,320,256]{2,1,0:T(8,128)S(1)} %get-tuple-element.15.sum_ref, f32[5,256,256]{2,1,0:T(8,128)S(1)} %copy-done.4, f32[5,8,256]{2,1,0:T(8,128)S(1)} %get-tuple-element.17.joint_ref, f32[256,256]{1,0:T(8,128)S(1)} %copy-done.8), custom_call_target="tpu_custom_call" | custom-call | flops 4194304 | bytes 4194 | tf_op jit(solution)/shard_map/pallas_call | solution.py:482
  73.5 0.0 collective-permute-done.2.left_ref
  73.5 0.0 collective-permute-done.3.right_ref
  73.5 0.0 copy-done.10
  73.5 2.7 %shard_map.114 = f32[5,256,256]{2,1,0:T(8,128)} custom-call(f32[5,256,256]{2,1,0:T(8,128)S(1)} %shard_map.112.inner_ref, f32[256,256]{1,0:T(8,128)S(1)} %copy-done.5, f32[5,8,512]{2,1,0:T(8,128)S(1)} %collective-permute-done.prior_ref, f32[5,8,512]{2,1,0:T(8,128)S(1)} %collective-permute-done.1.next_ref, f32[5,8,256]{2,1,0:T(8,128)S(1)} %collective-permute-done.2.left_ref, ...), custom_call_target="tpu_custom_call" | custom-call | tf_op jit(solution)/shard_map/pallas_call | solution.py:487
  (1 shorter events, 0.0 us)
Async XLA Ops:
  0.0 1.3 %copy-start = (f32[5,256,256]{2,1,0:T(8,128)S(1)}, f32[5,256,256]{2,1,0:T(8,128)}, u32[]{:S(2)}) copy-start(f32[5,256,256]{2,1,0:T(8,128)} %face_ref.3) | copy-start | bytes 3932164
  1.3 1.2 %copy-start.6 = (f32[5,32768]{1,0:T(8,128)S(1)}, f32[5,32768]{1,0:T(8,128)}, u32[]{:S(2)}) copy-start(f32[5,32768]{1,0:T(8,128)} %src_ref.1) | copy-start | bytes 1966084
  2.5 0.9 %copy-start.9 = (s32[32768]{0:T(1024)S(1)}, s32[32768]{0:T(1024)}, u32[]{:S(2)}) copy-start(s32[32768]{0:T(1024)} %param.14) | copy-start | bytes 393220
  3.4 0.7 copy-start.14
  8.2 1.0 %copy-start.2 = (f32[2304,128]{1,0:T(8,128)}, f32[2304,128]{1,0:T(8,128)S(1)}, u32[]{:S(2)}) copy-start(f32[2304,128]{1,0:T(8,128)S(1)} %shard_map.109) | copy-start | bytes 3538948
  9.3 4.7 %copy-start.1 = (f32[5,256,256]{2,1,0:T(8,128)S(1)}, f32[5,256,256]{2,1,0:T(8,128)}, u32[]{:S(2)}) copy-start(f32[5,256,256]{2,1,0:T(8,128)} %face_ref.3) | copy-start | bytes 3932164
  9.3 4.7 %copy-start.5 = (f32[256,256]{1,0:T(8,128)S(1)}, f32[256,256]{1,0:T(8,128)}, u32[]{:S(2)}) copy-start(f32[256,256]{1,0:T(8,128)} %kappa_ref.3) | copy-start | bytes 786436
  9.3 19.9 %all-to-all-start = ((f32[8,288,128]{2,1,0:T(8,128)}), f32[8,288,128]{2,1,0:T(8,128)S(1)}, u32[]{:S(2)}, u32[]{:S(2)}) async-start(f32[8,288,128]{2,1,0:T(8,128)} %bitcast.2), calls=%async_computation | async-start | bytes 2359296 | tf_op jit(solution)/shard_map/all_to_all | solution.py:462
  14.0 15.2 %copy-start.7 = (f32[256,512]{1,0:T(8,128)S(1)}, f32[256,512]{1,0:T(8,128)}, u32[]{:S(2)}) copy-start(f32[256,512]{1,0:T(8,128)} %constant.9.clone.far_ref) | copy-start | bytes 1572868
  14.0 15.2 %copy-start.11 = (f32[16,256]{1,0:T(8,128)S(1)}, f32[16,256]{1,0:T(8,128)}, u32[]{:S(2)}) copy-start(f32[16,256]{1,0:T(8,128)} %constant.8.clone.near_ref) | copy-start | bytes 49156
  14.0 15.2 %copy-start.12 = (s32[8]{0:T(128)S(1)}, s32[8]{0:T(128)}, u32[]{:S(2)}) copy-start(s32[8]{0:T(128)} %map_ref.1) | copy-start | bytes 100
  14.0 15.2 %copy-start.13 = (s32[8]{0:T(128)S(1)}, s32[8]{0:T(128)}, u32[]{:S(2)}) copy-start(s32[8]{0:T(128)} %match_ref.1) | copy-start | bytes 100
  15.4 1.1 %copy-start.3 = (f32[5,256,256]{2,1,0:T(8,128)}, f32[5,256,256]{2,1,0:T(8,128)S(1)}, u32[]{:S(2)}) copy-start(f32[5,256,256]{2,1,0:T(8,128)S(1)} %get-tuple-element.16.base_ref) | copy-start | bytes 3932164
  29.2 40.8 %copy-start.4 = (f32[5,256,256]{2,1,0:T(8,128)S(1)}, f32[5,256,256]{2,1,0:T(8,128)}, u32[]{:S(2)}) copy-start(f32[5,256,256]{2,1,0:T(8,128)} %copy-done.3) | copy-start | bytes 3932164
  29.2 40.8 %copy-start.8 = (f32[256,256]{1,0:T(8,128)S(1)}, f32[256,256]{1,0:T(8,128)}, u32[]{:S(2)}) copy-start(f32[256,256]{1,0:T(8,128)} %constant.10.clone.band_ref) | copy-start | bytes 786436
  53.0 5.4 %collective-permute-start = (f32[5,8,512]{2,1,0:T(8,128)S(1)}, f32[5,8,512]{2,1,0:T(8,128)S(1)}, u32[]{:S(2)}, u32[]{:S(2)}) collective-permute-start(f32[5,8,512]{2,1,0:T(8,128)S(1)} %get-tuple-element.18), channel_id=1, source_target_pairs={{0,4},{4,8},{8,12},{12,16},{16,20},{20,24},{24,28},{1,5},{5,9},{9,... | collective-permute-start | bytes 245768 | tf_op jit(solution)/shard_map/ppermute | solution.py:438
  56.5 6.7 %collective-permute-start.1 = (f32[5,8,512]{2,1,0:T(8,128)S(1)}, f32[5,8,512]{2,1,0:T(8,128)S(1)}, u32[]{:S(2)}, u32[]{:S(2)}) collective-permute-start(f32[5,8,512]{2,1,0:T(8,128)S(1)} %get-tuple-element.19), channel_id=1, source_target_pairs={{4,0},{8,4},{12,8},{16,12},{20,16},{24,20},{28,24},{5,1},{9,5},{13... | collective-permute-start | bytes 245768 | tf_op jit(solution)/shard_map/ppermute | solution.py:438
  63.1 10.3 %collective-permute-start.2 = (f32[5,8,256]{2,1,0:T(8,128)S(1)}, f32[5,8,256]{2,1,0:T(8,128)S(1)}, u32[]{:S(2)}, u32[]{:S(2)}) collective-permute-start(f32[5,8,256]{2,1,0:T(8,128)S(1)} %get-tuple-element.21), channel_id=1, source_target_pairs={{0,1},{1,2},{2,3},{4,5},{5,6},{6,7},{8,9},{9,10},{10,11},{12,13},{... | collective-permute-start | bytes 122888 | tf_op jit(solution)/shard_map/ppermute | solution.py:438
  68.1 5.4 %collective-permute-start.3 = (f32[5,8,256]{2,1,0:T(8,128)S(1)}, f32[5,8,256]{2,1,0:T(8,128)S(1)}, u32[]{:S(2)}, u32[]{:S(2)}) collective-permute-start(f32[5,8,256]{2,1,0:T(8,128)S(1)} %get-tuple-element.22), channel_id=1, source_target_pairs={{1,0},{2,1},{3,2},{5,4},{6,5},{7,6},{9,8},{10,9},{11,10},{13,12},{... | collective-permute-start | bytes 122888 | tf_op jit(solution)/shard_map/ppermute | solution.py:438
  70.0 3.5 %copy-start.10 = (f32[16,512]{1,0:T(8,128)S(1)}, f32[16,512]{1,0:T(8,128)}, u32[]{:S(2)}) copy-start(f32[16,512]{1,0:T(8,128)} %constant.11.clone.pick_ref) | copy-start | bytes 98308
